TPU v7x, 256 devices: a whole 4x4x8 slice. The times are simulated.
256 devices in a mesh: dp: 4 (over y), wide: 16 (over x_hi, z), narrow: 4 (over x_lo, core).
Axes of the slice: x: 4 (x_hi: 2, x_lo: 2; x = x_hi * 2 + x_lo), y: 4, z: 8, core: 2. Of those that a mesh axis runs over, the one named last changes fastest.
Arguments:
- tokens: bfloat16 [512, 256, 1280], P(('dp', 'wide', 'narrow')), may hold values from -20 to 20
- router: bfloat16 [1280, 128], replicated, may hold values from -1 to 1
- expert_in: bfloat16 [64, 1280, 2560], P(('wide', 'narrow'), None, 'dp'), may hold values from -0.15625 to 0.15625
- expert_out: bfloat16 [64, 2560, 1280], P(('wide', 'narrow'), 'dp'), may hold values from -0.125 to 0.125
- cotangent: bfloat16 [512, 256, 1280], P(('dp', 'wide', 'narrow')), may hold values from -6 to 6
Outputs:
- mixed: bfloat16 [512, 256, 1280], P(('dp', 'wide', 'narrow'))
- token_grad: bfloat16 [512, 256, 1280], P(('dp', 'wide', 'narrow'))
- router_grad: float32 [1280, 128], replicated
- grad_in: bfloat16 [64, 1280, 2560], P(('wide', 'narrow'), None, 'dp')
- grad_out: bfloat16 [64, 2560, 1280], P(('wide', 'narrow'), 'dp')
All inputs are finite; a program needn't handle non-finite values.
Results may differ from a plain program's by a relative error of at most 0.018.
Values may be sent and summed in bfloat16 or wider, within the bound.
A program may use at most 128 MiB of HBM per device.

v0:
```python
import jax
import jax.numpy as jnp
from jax import lax
from jax.sharding import PartitionSpec as P


def gelu_exact(values):
    return jax.nn.gelu(values, approximate=False)


def run_experts(expert_rows, expert_cots, expert_in, expert_out):
    w_first, w_second = (
        lax.all_gather(expert_in[0], "dp", axis=1, tiled=True),
        lax.all_gather(expert_out[0], "dp", axis=0, tiled=True),
    )
    pre = jnp.dot(expert_rows, w_first, preferred_element_type=jnp.float32)
    active, pullback = jax.vjp(gelu_exact, pre)
    act_low = active.astype(jnp.bfloat16)
    slot_out = jnp.dot(act_low, w_second, preferred_element_type=jnp.float32).astype(jnp.bfloat16)
    back = jnp.dot(expert_cots, w_second.T, preferred_element_type=jnp.float32)
    hidden_grad = pullback(back)[0].astype(jnp.bfloat16)
    slot_grad = jnp.dot(hidden_grad, w_first.T, preferred_element_type=jnp.float32).astype(
        jnp.bfloat16
    )
    term_first = jnp.dot(expert_rows.T, hidden_grad, preferred_element_type=jnp.float32)
    term_second = jnp.dot(act_low.T, expert_cots, preferred_element_type=jnp.float32)
    grad_first, grad_second = (
        lax.psum_scatter(
            term_first.astype(jnp.bfloat16), "dp", scatter_dimension=1, tiled=True
        ).astype(jnp.float32),
        lax.psum_scatter(
            term_second.astype(jnp.bfloat16), "dp", scatter_dimension=0, tiled=True
        ).astype(jnp.float32),
    )
    grad_first = grad_first.astype(jnp.bfloat16)
    grad_second = grad_second.astype(jnp.bfloat16)
    return (slot_out, slot_grad, grad_first[None], grad_second[None])


def local(tokens, router, expert_in, expert_out, cotangent):
    images, length, width = tokens.shape
    slot_count = router.shape[1]
    n_wide = lax.axis_size("wide")
    n_narrow = lax.axis_size("narrow")
    per_expert = slot_count // (n_wide * n_narrow)
    logits = jnp.einsum("itd,ds->its", tokens, router, preferred_element_type=jnp.float32)
    dispatch = jax.nn.softmax(logits, axis=1)
    combine = jax.nn.softmax(logits, axis=2)
    dispatch_low = dispatch.astype(jnp.bfloat16)
    combine_low = combine.astype(jnp.bfloat16)
    slot_in = jnp.einsum(
        "its,itd->sid", dispatch_low, tokens, preferred_element_type=jnp.float32
    ).astype(jnp.bfloat16)
    slot_cot = jnp.einsum(
        "its,itd->sid", combine_low, cotangent, preferred_element_type=jnp.float32
    ).astype(jnp.bfloat16)
    shape_four = (n_wide * n_narrow, per_expert, images, width)
    rows_in, cots_in = (
        lax.all_to_all(
            slot_in.reshape(shape_four), ("wide", "narrow"), split_axis=0, concat_axis=0, tiled=True
        ),
        lax.all_to_all(
            slot_cot.reshape(shape_four),
            ("wide", "narrow"),
            split_axis=0,
            concat_axis=0,
            tiled=True,
        ),
    )
    slot_out, slot_grad, grad_in, grad_out = run_experts(
        rows_in.reshape(-1, width), cots_in.reshape(-1, width), expert_in, expert_out
    )
    outs_back, grads_back = (
        lax.all_to_all(
            slot_out.reshape(shape_four),
            ("wide", "narrow"),
            split_axis=0,
            concat_axis=0,
            tiled=True,
        ),
        lax.all_to_all(
            slot_grad.reshape(shape_four),
            ("wide", "narrow"),
            split_axis=0,
            concat_axis=0,
            tiled=True,
        ),
    )
    outs_back = outs_back.reshape(slot_count, images, width)
    grads_back = grads_back.reshape(slot_count, images, width)
    mixed = jnp.einsum(
        "its,sid->itd", combine_low, outs_back, preferred_element_type=jnp.float32
    ).astype(jnp.bfloat16)
    left = jnp.einsum("itd,sid->its", cotangent, outs_back, preferred_element_type=jnp.float32)
    right = jnp.einsum("itd,sid->its", tokens, grads_back, preferred_element_type=jnp.float32)
    part_combine = combine * (left - jnp.sum(combine * left, axis=2, keepdims=True))
    part_dispatch = dispatch * (right - jnp.sum(dispatch * right, axis=1, keepdims=True))
    logit_grad = (part_combine + part_dispatch).astype(jnp.bfloat16)
    token_grad = jnp.einsum(
        "its,sid->itd", dispatch_low, grads_back, preferred_element_type=jnp.float32
    )
    token_grad = token_grad + jnp.einsum(
        "its,ds->itd", logit_grad, router, preferred_element_type=jnp.float32
    )
    router_local = jnp.einsum("itd,its->ds", tokens, logit_grad, preferred_element_type=jnp.float32)
    router_grad = lax.psum(router_local, ("dp", "wide", "narrow"))
    return (mixed, token_grad.astype(jnp.bfloat16), router_grad, grad_in, grad_out)


def solution(mesh):
    in_specs = (
        P(("dp", "wide", "narrow"), None, None),
        P(),
        P(("wide", "narrow"), None, "dp"),
        P(("wide", "narrow"), "dp", None),
        P(("dp", "wide", "narrow"), None, None),
    )
    out_specs = (
        P(("dp", "wide", "narrow"), None, None),
        P(("dp", "wide", "narrow"), None, None),
        P(),
        P(("wide", "narrow"), None, "dp"),
        P(("wide", "narrow"), "dp", None),
    )
    return jax.shard_map(local, mesh=mesh, in_specs=in_specs, out_specs=out_specs, check_vma=False)
```

profile of v0, /device:TPU:1, one launch (start us, length us, event | category | flops | bytes accessed | tf_op | source)
XLA Modules:
  0.0 624.6 jit_solution(4454238204223516543)
XLA Ops:
  7.2 0.0 copy-start
  7.2 0.0 copy-start.1
  7.2 0.0 copy-start.6
  7.2 0.0 all-gather.5.cloned.1.call-start
  7.2 0.7 all-gather.5.cloned.1.call-update
  7.9 0.0 all-gather.7.cloned.1.call-start
  8.0 0.7 all-gather.7.cloned.1.call-update
  8.7 0.0 copy-done
  8.7 0.0 copy-done.1
  8.7 0.5 fusion.49
  9.2 0.8 fusion.60
  10.1 0.0 copy-done.6
  10.1 1.2 fusion.28
  11.3 1.5 copy.45
  12.8 13.0 %all-to-all-start.2 = ((bf16[64,2,2,1280]{3,2,1,0:T(2,128)(2,1)}), bf16[64,2,2,1280]{3,2,1,0:T(2,128)(2,1)S(1)}, u32[]{:S(2)}, u32[]{:S(2)}) async-start(bf16[64,2,2,1280]{3,2,1,0:T(2,128)(2,1)} %bitcast.7), calls=%async_computation.2 | async-start | bytes 1310720 | tf_op jit(solution)/shard_map/all_to_all | solution.py:62
  25.8 0.8 fusion.59
  26.6 0.4 fusion.27
  27.0 1.5 copy.43
  28.5 17.4 %all-to-all-done.2 = bf16[64,2,2,1280]{3,2,1,0:T(2,128)(2,1)S(1)} async-done(((bf16[64,2,2,1280]{3,2,1,0:T(2,128)(2,1)}), bf16[64,2,2,1280]{3,2,1,0:T(2,128)(2,1)S(1)}, u32[]{:S(2)}, u32[]{:S(2)}) %all-to-all-start.2) | async-done | bytes 655392 | tf_op jit(solution)/shard_map/all_to_all | solution.py:62
  45.9 6.1 all-to-all-start
  52.1 0.2 reshape.45
  52.3 19.9 %all-to-all-done = bf16[64,2,2,1280]{3,2,1,0:T(2,128)(2,1)S(1)} async-done(((bf16[64,2,2,1280]{3,2,1,0:T(2,128)(2,1)}), bf16[64,2,2,1280]{3,2,1,0:T(2,128)(2,1)S(1)}, u32[]{:S(2)}, u32[]{:S(2)}) %all-to-all-start) | async-done | bytes 655392 | tf_op jit(solution)/shard_map/all_to_all | solution.py:59
  72.2 0.2 reshape.41
  72.5 11.6 %all-gather.5.cloned.1.call-done = bf16[1,1280,2560]{2,1,0:T(8,128)(2,1)} async-done(((bf16[1,1280,640]{2,1,0:T(8,128)(2,1)}), bf16[1,1280,2560]{2,1,0:T(8,128)(2,1)}) %all-gather.5.cloned.1.call-update) | async-done | bytes 6553616 | tf_op jit(solution)/shard_map/all_gather | solution.py:13
  84.1 10.7 %multiply_convert_fusion = (bf16[256,2560]{1,0:T(8,128)(2,1)}, f32[256,2560]{1,0:T(8,128)}, f32[256,2560]{1,0:T(8,128)}) fusion(bf16[256,1280]{1,0:T(8,128)(2,1)S(1)} %reshape.41, bf16[1,1280,2560]{2,1,0:T(8,128)(2,1)} %all-gather.5.cloned.1.call-done), kind=kOutput, calls=%fused_computation.20 | convolution fusion | flops 1720320000 | bytes 13762560 | tf_op jit(solution)/shard_map/dot_general | solution.py:16
  94.8 62.3 %all-gather.7.cloned.1.call-done = bf16[1,2560,1280]{2,1,0:T(8,128)(2,1)} async-done(((bf16[1,640,1280]{2,1,0:T(8,128)(2,1)}), bf16[1,2560,1280]{2,1,0:T(8,128)(2,1)}) %all-gather.7.cloned.1.call-update) | async-done | bytes 6553616 | tf_op jit(solution)/shard_map/all_gather | solution.py:14
  157.1 5.1 fusion.24
  162.3 1.1 reshape.42
  163.3 10.7 %all-to-all-start.1 = ((bf16[64,2,2,1280]{3,2,1,0:T(2,128)(2,1)}), bf16[64,2,2,1280]{3,2,1,0:T(2,128)(2,1)S(1)}, u32[]{:S(2)}, u32[]{:S(2)}) async-start(bf16[64,2,2,1280]{3,2,1,0:T(2,128)(2,1)} %reshape.42), calls=%async_computation.1 | async-start | bytes 1310720 | tf_op jit(solution)/shard_map/all_to_all | solution.py:74
  174.0 7.8 %add_convert_fusion = bf16[256,2560]{1,0:T(8,128)(2,1)} fusion(f32[256,2560]{1,0:T(8,128)} %get-tuple-element.21, bf16[256,1280]{1,0:T(8,128)(2,1)S(1)} %reshape.45, bf16[1,2560,1280]{2,1,0:T(8,128)(2,1)} %all-gather.7.cloned.1.call-done, f32[256,2560]{1,0:T(8,128)} %get-tuple-element.24), kind=kOutput, calls=%fused_computation.19 | convolution fusion | flops 1686896640 | bytes 13762560 | tf_op jit(solution)/shard_map/dot_general | solution.py:20
  181.8 6.0 fusion.21
  187.8 2.6 reshape.46
  190.5 3.8 all-to-all-done.1
  194.2 0.0 copy-start.4
  194.2 0.8 copy-done.4
  195.0 6.6 %all-to-all-start.3 = ((bf16[64,2,2,1280]{3,2,1,0:T(2,128)(2,1)}), bf16[64,2,2,1280]{3,2,1,0:T(2,128)(2,1)S(1)}, u32[]{:S(2)}, u32[]{:S(2)}) async-start(bf16[64,2,2,1280]{3,2,1,0:T(2,128)(2,1)} %reshape.46), calls=%async_computation.3 | async-start | bytes 1310720 | tf_op jit(solution)/shard_map/all_to_all | solution.py:81
  201.7 0.0 all-reduce.2.cloned.1.call-start
  201.7 2.7 convolution_bitcast_fusion.2
  204.5 17.4 %all-to-all-done.3 = bf16[64,2,2,1280]{3,2,1,0:T(2,128)(2,1)S(1)} async-done(((bf16[64,2,2,1280]{3,2,1,0:T(2,128)(2,1)}), bf16[64,2,2,1280]{3,2,1,0:T(2,128)(2,1)S(1)}, u32[]{:S(2)}, u32[]{:S(2)}) %all-to-all-start.3) | async-done | bytes 655392 | tf_op jit(solution)/shard_map/all_to_all | solution.py:81
  221.9 0.5 convolution_bitcast_fusion.1
  222.4 1.8 fusion.35
  224.2 4.7 convolution_bitcast_fusion
  228.9 0.0 all-reduce.2.cloned.1.call-update
  228.9 0.0 reduce-scatter.7.cloned.1.call-start
  228.9 6.0 convolution_convert_fusion.1
  234.9 9.4 %copy.47 = bf16[1280,2560]{0,1:T(8,128)(2,1)} copy(bf16[1280,2560]{1,0:T(8,128)(2,1)} %convolution_convert_fusion.1) | data formatting | bytes 13107200
  244.4 0.0 reduce-scatter.7.cloned.1.call-update
  244.4 0.3 reduce-scatter.5.cloned.1.call-start
  244.7 6.0 convolution_convert_fusion
  250.7 0.0 copy-start.5
  250.7 0.0 reduce-scatter.5.cloned.1.call-update
  250.7 1.1 copy-done.5
  251.8 0.0 copy-start.2
  251.8 0.0 copy-start.3
  251.8 2.3 convolution_convert_fusion.2
  254.1 2.0 fusion.40
  256.1 0.0 copy-done.2
  256.1 0.0 copy-done.3
  256.1 5.4 fusion.12
  261.5 215.3 %all-reduce.2.cloned.1.call-done = f32[1280,128]{0,1:T(8,128)} async-done(((f32[1280,128]{0,1:T(8,128)}), f32[1280,128]{0,1:T(8,128)}) %all-reduce.2.cloned.1.call-update) | async-done | bytes 655376 | tf_op jit(solution)/shard_map/psum | solution.py:106
  476.8 2.2 copy.37
  478.9 67.6 %reduce-scatter.7.cloned.1.call-done = bf16[640,1280]{1,0:T(8,128)(2,1)} async-done(((bf16[2560,1280]{1,0:T(8,128)(2,1)}), bf16[640,1280]{1,0:T(8,128)(2,1)}) %reduce-scatter.7.cloned.1.call-update) | async-done | bytes 1638416
  546.5 3.5 copy.48
  550.0 68.1 %reduce-scatter.5.cloned.1.call-done = bf16[640,1280]{1,0:T(8,128)(2,1)} async-done(((bf16[2560,1280]{1,0:T(8,128)(2,1)}), bf16[640,1280]{1,0:T(8,128)(2,1)}) %reduce-scatter.5.cloned.1.call-update) | async-done | bytes 1638416 | tf_op jit(solution)/shard_map/reduce_scatter | solution.py:31
Async XLA Ops:
  7.2 1.5 copy-start
  7.2 1.5 copy-start.1
  7.2 2.9 copy-start.6
  7.2 76.9 %all-gather.5.cloned.1.call-start = ((), (), s32[]{:S(2)}) async-start(), calls=%async_computation.8 | async-start | bytes 8192000 | tf_op jit(solution)/shard_map/all_gather | solution.py:13
  7.9 149.2 %all-gather.7.cloned.1.call-start = ((), (), s32[]{:S(2)}) async-start(), calls=%async_computation.9 | async-start | bytes 8192000 | tf_op jit(solution)/shard_map/all_gather | solution.py:14
  12.8 33.2 %all-to-all-start.2 = ((bf16[64,2,2,1280]{3,2,1,0:T(2,128)(2,1)}), bf16[64,2,2,1280]{3,2,1,0:T(2,128)(2,1)S(1)}, u32[]{:S(2)}, u32[]{:S(2)}) async-start(bf16[64,2,2,1280]{3,2,1,0:T(2,128)(2,1)} %bitcast.7), calls=%async_computation.2 | async-start | bytes 1310720 | tf_op jit(solution)/shard_map/all_to_all | solution.py:62
  45.9 26.3 %all-to-all-start = ((bf16[64,2,2,1280]{3,2,1,0:T(2,128)(2,1)}), bf16[64,2,2,1280]{3,2,1,0:T(2,128)(2,1)S(1)}, u32[]{:S(2)}, u32[]{:S(2)}) async-start(bf16[64,2,2,1280]{3,2,1,0:T(2,128)(2,1)} %bitcast.2), calls=%async_computation | async-start | bytes 1310720 | tf_op jit(solution)/shard_map/all_to_all | solution.py:59
  163.3 30.9 %all-to-all-start.1 = ((bf16[64,2,2,1280]{3,2,1,0:T(2,128)(2,1)}), bf16[64,2,2,1280]{3,2,1,0:T(2,128)(2,1)S(1)}, u32[]{:S(2)}, u32[]{:S(2)}) async-start(bf16[64,2,2,1280]{3,2,1,0:T(2,128)(2,1)} %reshape.42), calls=%async_computation.1 | async-start | bytes 1310720 | tf_op jit(solution)/shard_map/all_to_all | solution.py:74
  194.2 0.8 copy-start.4
  195.0 26.8 %all-to-all-start.3 = ((bf16[64,2,2,1280]{3,2,1,0:T(2,128)(2,1)}), bf16[64,2,2,1280]{3,2,1,0:T(2,128)(2,1)S(1)}, u32[]{:S(2)}, u32[]{:S(2)}) async-start(bf16[64,2,2,1280]{3,2,1,0:T(2,128)(2,1)} %reshape.46), calls=%async_computation.3 | async-start | bytes 1310720 | tf_op jit(solution)/shard_map/all_to_all | solution.py:81
  201.7 275.1 %all-reduce.2.cloned.1.call-start = ((), (), s32[]{:S(2)}) async-start(), calls=%async_computation.6 | async-start | bytes 1310720 | tf_op jit(solution)/shard_map/psum | solution.py:106
  228.9 317.6 %reduce-scatter.7.cloned.1.call-start = ((), (), s32[]{:S(2)}) async-start(), calls=%async_computation.10 | async-start | bytes 8192000
  244.4 373.7 %reduce-scatter.5.cloned.1.call-start = ((), (), s32[]{:S(2)}) async-start(), calls=%async_computation.7 | async-start | bytes 8192000 | tf_op jit(solution)/shard_map/reduce_scatter | solution.py:31
  250.7 1.1 copy-start.5
  251.8 4.3 copy-start.2
  251.8 4.3 copy-start.3
Sparse Core Ops, SparseCore 0:
  9.9 74.2 all-gather.4
  85.9 71.1 all-gather.6
  229.0 247.7 all-reduce.1
  479.3 67.0 reduce-scatter.6
  549.6 68.4 reduce-scatter.4
where the time goes:
time: 626 us; the launch traced here: 625 us
  waiting for transfers between devices  485 us (77%)
  matrix products  61.4 us (10%)
  starting transfers between devices  36.8 us (6%)
  local copies, waits for them, and re-layouts  24.3 us (4%)
  between operations  13.9 us (2%)
    psum x1, waiting for transfers between devices, local(): router_grad = lax.psum(router_local, ('dp', 'wide', 'narrow'))  215 us
    unnamed x6, waiting for transfers between devices  69 us
    reduce_scatter x1, waiting for transfers between devices, run_experts(): lax.psum_scatter(term_second.astype(jnp.bfloat16), 'dp', scatter_dimensio...  68.1 us
    all_gather x1, waiting for transfers between devices, run_experts(): lax.all_gather(expert_out[0], 'dp', axis=0, tiled=True)  62.3 us
    all_to_all x1, waiting for transfers between devices, local(): lax.all_to_all(slot_in.reshape(shape_four), ('wide', 'narrow'), split_axi...  19.9 us
    all_to_all x1, waiting for transfers between devices, local(): lax.all_to_all(slot_cot.reshape(shape_four), ('wide', 'narrow'), split_ax...  17.4 us
    all_to_all x1, waiting for transfers between devices, local(): lax.all_to_all(slot_grad.reshape(shape_four), ('wide', 'narrow'), split_a...  17.4 us
    unnamed x17, local copies, waits for them, and re-layouts  17 us
  transfers between devices with their start and end apart: 9, of which 9 were waited for; matrix products, arithmetic and copies ran while one was open for 12% of the time, Pallas kernels for 0%

commit v1 on v0

v1 whole, which is shorter than its diff:
```python
import jax
import jax.numpy as jnp
from jax import lax
from jax.sharding import PartitionSpec as P

PLANE = ("wide", "narrow")


def gelu_exact(values):
    return jax.nn.gelu(values, approximate=False)


def dot(a, b):
    return jnp.dot(a, b, preferred_element_type=jnp.float32)


def exchange(x):
    return lax.all_to_all(x, PLANE, split_axis=0, concat_axis=0, tiled=True)


def local(tokens, router, expert_in, expert_out, cotangent):
    images, length, width = tokens.shape
    slot_count = router.shape[1]
    n_plane = lax.axis_size("wide") * lax.axis_size("narrow")
    n_dp = lax.axis_size("dp")
    per_expert = slot_count // n_plane
    logits = jnp.einsum("itd,ds->its", tokens, router, preferred_element_type=jnp.float32)
    dispatch = jax.nn.softmax(logits, axis=1)
    combine = jax.nn.softmax(logits, axis=2)
    dispatch_low = dispatch.astype(jnp.bfloat16)
    combine_low = combine.astype(jnp.bfloat16)
    slot_in = jnp.einsum(
        "its,itd->sid", dispatch_low, tokens, preferred_element_type=jnp.float32
    ).astype(jnp.bfloat16)
    slot_cot = jnp.einsum(
        "its,itd->sid", combine_low, cotangent, preferred_element_type=jnp.float32
    ).astype(jnp.bfloat16)
    shape = (n_plane, per_expert * images, width)
    rows = lax.all_gather(exchange(slot_in.reshape(shape)).reshape(-1, width), "dp", axis=0, tiled=True)
    cots = lax.all_gather(exchange(slot_cot.reshape(shape)).reshape(-1, width), "dp", axis=0, tiled=True)

    first, second = expert_in[0], expert_out[0]
    pre = dot(rows, first)
    active, pullback = jax.vjp(gelu_exact, pre)
    act_low = active.astype(jnp.bfloat16)
    out_part = dot(act_low, second).astype(jnp.bfloat16)
    slot_out = lax.psum_scatter(out_part, "dp", scatter_dimension=0, tiled=True)
    back = lax.dot_general(cots, second, (((1,), (1,)), ((), ())), preferred_element_type=jnp.float32)
    hidden_grad = pullback(back)[0].astype(jnp.bfloat16)
    grad_part = lax.dot_general(
        hidden_grad, first, (((1,), (1,)), ((), ())), preferred_element_type=jnp.float32
    ).astype(jnp.bfloat16)
    slot_grad = lax.psum_scatter(grad_part, "dp", scatter_dimension=0, tiled=True)
    grad_in = lax.dot_general(
        rows, hidden_grad, (((0,), (0,)), ((), ())), preferred_element_type=jnp.float32
    ).astype(jnp.bfloat16)
    grad_out = lax.dot_general(
        act_low, cots, (((0,), (0,)), ((), ())), preferred_element_type=jnp.float32
    ).astype(jnp.bfloat16)

    outs_back = exchange(slot_out.reshape(shape)).reshape(slot_count, images, width)
    grads_back = exchange(slot_grad.reshape(shape)).reshape(slot_count, images, width)
    mixed = jnp.einsum(
        "its,sid->itd", combine_low, outs_back, preferred_element_type=jnp.float32
    ).astype(jnp.bfloat16)
    left = jnp.einsum("itd,sid->its", cotangent, outs_back, preferred_element_type=jnp.float32)
    right = jnp.einsum("itd,sid->its", tokens, grads_back, preferred_element_type=jnp.float32)
    part_combine = combine * (left - jnp.sum(combine * left, axis=2, keepdims=True))
    part_dispatch = dispatch * (right - jnp.sum(dispatch * right, axis=1, keepdims=True))
    logit_grad = (part_combine + part_dispatch).astype(jnp.bfloat16)
    token_grad = jnp.einsum(
        "its,sid->itd", dispatch_low, grads_back, preferred_element_type=jnp.float32
    )
    token_grad = token_grad + jnp.einsum(
        "its,ds->itd", logit_grad, router, preferred_element_type=jnp.float32
    )
    router_local = jnp.einsum("itd,its->ds", tokens, logit_grad, preferred_element_type=jnp.float32)
    share = exchange(router_local.reshape(n_plane, -1, slot_count))
    share = lax.psum(jnp.sum(share, axis=0), "dp")
    router_grad = lax.all_gather(share, PLANE, axis=0, tiled=True)
    return (mixed, token_grad.astype(jnp.bfloat16), router_grad, grad_in[None], grad_out[None])


def solution(mesh):
    in_specs = (
        P(("dp", "wide", "narrow"), None, None),
        P(),
        P(("wide", "narrow"), None, "dp"),
        P(("wide", "narrow"), "dp", None),
        P(("dp", "wide", "narrow"), None, None),
    )
    out_specs = (
        P(("dp", "wide", "narrow"), None, None),
        P(("dp", "wide", "narrow"), None, None),
        P(),
        P(("wide", "narrow"), None, "dp"),
        P(("wide", "narrow"), "dp", None),
    )
    return jax.shard_map(local, mesh=mesh, in_specs=in_specs, out_specs=out_specs, check_vma=False)
```

time: 626 us -> 384 us (0.61)
  waiting for transfers between devices: 485 us -> 107 us
  blocking collectives: 0 us -> 149 us
  starting transfers between devices: 36.8 us -> 27.8 us
    psum x1 -> x0, waiting for transfers between devices: 215 us -> none  [local(): router_grad = lax.psum(router_local, ('dp', 'wide', 'narrow'))]
    all_gather x0 -> x1, blocking collectives: none -> 79.3 us  [local(): router_grad = lax.all_gather(share, PLANE, axis=0, tiled=True)]
    unnamed x6 -> x4, waiting for transfers between devices: 69 us -> 0.07 us
    all_to_all x0 -> x2, blocking collectives: none -> 59 us  [exchange(): return lax.all_to_all(x, PLANE, split_axis=0, concat_axis=0, tiled=True)]
    all_to_all x4 -> x3, waiting for transfers between devices: 58.5 us -> 15.7 us  [exchange(): return lax.all_to_all(x, PLANE, split_axis=0, concat_axis=0, tiled=True)]
    all_gather x2, waiting for transfers between devices: 73.9 us -> 33.3 us  [the longest x1 30.2 us: local(): lax.all_gather(exchange(slot_cot.reshape(shape)).reshape(-1, width), 'dp'...]
    unnamed x17 -> x13, local copies, waits for them, and re-layouts: 17 us -> 2.8 us
    psum x0 -> x1, blocking collectives: none -> 11.1 us  [local(): share = lax.psum(jnp.sum(share, axis=0), 'dp')]
  transfers between devices with their start and end apart: 9 -> 7, of which waited for: 9 -> 6; matrix products, arithmetic and copies ran while one was open for 12% -> 14% of each run, Pallas kernels for 0% -> 0%
where the time goes in v1:
time: 384 us; the launch traced here: 383 us
  blocking collectives  149 us (39%)
  waiting for transfers between devices  107 us (28%)
  matrix products  63.2 us (16%)
  starting transfers between devices  27.8 us (7%)
  local copies, waits for them, and re-layouts  18.7 us (5%)
  between operations  13.9 us (4%)
    all_gather x1, blocking collectives, local(): router_grad = lax.all_gather(share, PLANE, axis=0, tiled=True)  79.3 us
    all_to_all x2, blocking collectives, exchange(): return lax.all_to_all(x, PLANE, split_axis=0, concat_axis=0, tiled=True)  59 us
    reduce_scatter x1, waiting for transfers between devices, local(): lax.psum_scatter(grad_part, 'dp', scatter_dimension=0, tiled=True)  31.6 us
    all_gather x1, waiting for transfers between devices, local(): lax.all_gather(exchange(slot_cot.reshape(shape)).reshape(-1, width), 'dp'...  30.2 us
    all_to_all x3, starting transfers between devices, exchange(): return lax.all_to_all(x, PLANE, split_axis=0, concat_axis=0, tiled=True)  27.5 us
    reduce_scatter x1, waiting for transfers between devices, local(): slot_out = lax.psum_scatter(out_part, 'dp', scatter_dimension=0, tiled=True)  25.9 us
    all_to_all x3, waiting for transfers between devices, exchange(): return lax.all_to_all(x, PLANE, split_axis=0, concat_axis=0, tiled=True)  15.7 us
    dot_general x2, matrix products, dot(): return jnp.dot(a, b, preferred_element_type=jnp.float32)  15.3 us
  transfers between devices with their start and end apart: 7, of which 6 were waited for; matrix products, arithmetic and copies ran while one was open for 14% of the time, Pallas kernels for 0%

profile of v1, /device:TPU:1, one launch (start us, length us, event | category | flops | bytes accessed | tf_op | source)
XLA Modules:
  0.0 383.4 jit_solution(10028998244327278210)
XLA Ops:
  7.2 0.0 copy-start
  7.2 0.0 all-gather.4.cloned.1.call-start
  7.2 2.0 fusion.43
  9.2 0.8 fusion.53
  10.0 1.7 fusion.13
  11.7 0.7 copy.28
  12.4 0.3 reshape.43
  12.7 33.0 %all_to_all.25 = bf16[64,4,1280]{2,1,0:T(4,128)(2,1)S(1)} all-to-all(bf16[64,4,1280]{2,1,0:T(4,128)(2,1)S(1)} %reshape.43), channel_id=1, replica_groups=mesh['dp'=4,'wide'=16,'narrow'=4] {'wide','narrow'}, dimensions={0} | all-to-all | bytes 1310720 | tf_op jit(solution)/shard_map/all_to_all | solution.py:18
  45.6 1.0 reshape.44
  46.6 0.0 all-gather.4.cloned.1.call-update
  46.7 0.0 all-gather.6.cloned.1.call-start
  46.7 0.8 fusion.54
  47.6 2.5 fusion.14
  50.1 0.7 copy.31
  50.8 0.3 reshape.47
  51.0 26.1 %all_to_all.26 = bf16[64,4,1280]{2,1,0:T(4,128)(2,1)S(1)} all-to-all(bf16[64,4,1280]{2,1,0:T(4,128)(2,1)S(1)} %reshape.47), channel_id=1, replica_groups=mesh['dp'=4,'wide'=16,'narrow'=4] {'wide','narrow'}, dimensions={0} | all-to-all | bytes 1310720 | tf_op jit(solution)/shard_map/all_to_all | solution.py:18
  77.1 1.0 reshape.48
  78.1 0.0 all-gather.6.cloned.1.call-update
  78.1 0.2 reduce-scatter.5.cloned.1.call-start
  78.3 3.2 all-gather.4.cloned.1.call-done
  81.5 0.0 copy-done
  81.5 10.1 %multiply_convert_fusion = (bf16[1024,640]{1,0:T(8,128)(2,1)S(1)}, f32[1024,640]{1,0:T(8,128)}, f32[1024,640]{1,0:T(8,128)}) fusion(bf16[1024,1280]{1,0:T(8,128)(2,1)} %all-gather.4.cloned.1.call-done, bf16[1,1280,640]{2,1,0:T(8,128)(2,1)S(1)} %copy-done), kind=kOutput, calls=%fused_computation.16 | convolution fusion | flops 1720320000 | bytes 10813440 | tf_op jit(solution)/shard_map/dot_general | solution.py:14
  91.6 30.2 %all-gather.6.cloned.1.call-done = bf16[1024,1280]{1,0:T(8,128)(2,1)} async-done(((bf16[256,1280]{1,0:T(8,128)(2,1)}), bf16[1024,1280]{1,0:T(8,128)(2,1)}) %all-gather.6.cloned.1.call-update) | async-done | bytes 2621456 | tf_op jit(solution)/shard_map/all_gather | solution.py:40
  121.8 6.4 %add_convert_fusion = bf16[1024,640]{1,0:T(8,128)(2,1)S(1)} fusion(f32[1024,640]{1,0:T(8,128)} %get-tuple-element.6, f32[1024,640]{1,0:T(8,128)} %get-tuple-element.9, bf16[1024,1280]{1,0:T(8,128)(2,1)} %all-gather.6.cloned.1.call-done, bf16[1,640,1280]{2,1,0:T(8,128)(2,1)} %param.8), kind=kOutput, calls=%fused_computation.15 | convolution fusion | flops 1686896640 | bytes 10813440 | tf_op jit(solution)/shard_map/dot_general | solution.py:48
  128.2 0.0 copy-start.5
  128.2 1.0 copy-done.5
  129.2 3.8 convolution_convert_fusion
  133.0 0.0 reduce-scatter.5.cloned.1.call-update
  133.1 0.0 reduce-scatter.3.cloned.1.call-start
  133.1 0.0 copy-done.4
  133.1 5.1 %convolution_convert_fusion.1 = bf16[1024,1280]{1,0:T(8,128)(2,1)} fusion(bf16[1024,640]{1,0:T(8,128)(2,1)S(1)} %get-tuple-element.5, bf16[1,640,1280]{2,1,0:T(8,128)(2,1)} %param.8), kind=kOutput, calls=%fused_computation.6 | convolution fusion | flops 1679032320 | bytes 5570560 | tf_op jit(solution)/shard_map/dot_general | solution.py:14
  138.3 0.0 reduce-scatter.3.cloned.1.call-update
  138.3 31.6 %reduce-scatter.5.cloned.1.call-done = bf16[256,1280]{1,0:T(8,128)(2,1)} async-done(((bf16[1024,1280]{1,0:T(8,128)(2,1)}), bf16[256,1280]{1,0:T(8,128)(2,1)}) %reduce-scatter.5.cloned.1.call-update) | async-done | bytes 655376 | tf_op jit(solution)/shard_map/reduce_scatter | solution.py:53
  169.9 2.3 reshape.49
  172.2 10.6 %all-to-all-start.3 = ((bf16[64,4,1280]{2,1,0:T(4,128)(2,1)}), bf16[64,4,1280]{2,1,0:T(4,128)(2,1)S(1)}, u32[]{:S(2)}, u32[]{:S(2)}) async-start(bf16[64,4,1280]{2,1,0:T(4,128)(2,1)} %reshape.49), calls=%async_computation.5 | async-start | bytes 1310720 | tf_op jit(solution)/shard_map/all_to_all | solution.py:18
  182.8 25.9 %reduce-scatter.3.cloned.1.call-done = bf16[256,1280]{1,0:T(8,128)(2,1)} async-done(((bf16[1024,1280]{1,0:T(8,128)(2,1)}), bf16[256,1280]{1,0:T(8,128)(2,1)}) %reduce-scatter.3.cloned.1.call-update) | async-done | bytes 655376 | tf_op jit(solution)/shard_map/reduce_scatter | solution.py:47
  208.7 2.3 reshape.45
  210.9 0.0 all-to-all-done.3
  210.9 0.8 copy-done.2
  211.8 10.8 %all-to-all-start.1 = ((bf16[64,4,1280]{2,1,0:T(4,128)(2,1)}), bf16[64,4,1280]{2,1,0:T(4,128)(2,1)}, u32[]{:S(2)}, u32[]{:S(2)}) async-start(bf16[64,4,1280]{2,1,0:T(4,128)(2,1)} %reshape.45), calls=%async_computation.2 | async-start | bytes 1310720 | tf_op jit(solution)/shard_map/all_to_all | solution.py:18
  222.6 0.0 copy-start.1
  222.6 5.3 %fusion.6 = bf16[1,640,1280]{2,1,0:T(8,128)(2,1)} fusion(bf16[1024,640]{1,0:T(8,128)(2,1)} %copy-done.4, bf16[1024,1280]{1,0:T(8,128)(2,1)} %all-gather.6.cloned.1.call-done), kind=kOutput, calls=%fused_computation.13 | convolution fusion | flops 1678540800 | bytes 5570560 | tf_op jit(solution)/shard_map/dot_general | solution.py:57
  227.9 2.6 reshape.50
  230.5 0.0 copy-done.1
  230.5 2.3 convolution_bitcast_fusion.1
  232.8 9.9 %all-to-all-done.1 = bf16[64,4,1280]{2,1,0:T(4,128)(2,1)} async-done(((bf16[64,4,1280]{2,1,0:T(4,128)(2,1)}), bf16[64,4,1280]{2,1,0:T(4,128)(2,1)}, u32[]{:S(2)}, u32[]{:S(2)}) %all-to-all-start.1) | async-done | bytes 655392 | tf_op jit(solution)/shard_map/all_to_all | solution.py:18
  242.7 2.6 reshape.46
  245.3 2.7 convolution_bitcast_fusion.2
  248.0 2.0 fusion.29
  250.0 4.7 %convolution_bitcast_fusion = f32[1280,128]{0,1:T(8,128)} fusion(bf16[2,256,1280]{2,1,0:T(8,128)(2,1)S(1)} %copy-done.1, f32[2,256,128]{2,1,0:T(8,128)} %fusion.29, f32[2,256,128]{2,1,0:T(8,128)} %convolution_bitcast_fusion.2, f32[2,256,128]{2,1,0:T(8,128)} %get-tuple-element.11, f32[2,256]{1,0:T(2,128)S(1)} %get-tuple-element.10), kind=kOutput, calls=%fused_computation.34 | convolution fusion | flops 168231552 | bytes 2754560 | tf_op jit(solution)/shard_map/itd,its->ds/dot_general | solution.py:77
  254.7 1.3 copy.38
  256.0 0.9 reshape.51
  256.9 6.1 %all-to-all-start.4 = ((f32[64,20,128]{2,1,0:T(8,128)}), f32[64,20,128]{2,1,0:T(8,128)S(1)}, u32[]{:S(2)}, u32[]{:S(2)}) async-start(f32[64,20,128]{2,1,0:T(8,128)} %reshape.51), calls=%async_computation.6 | async-start | bytes 1572864 | tf_op jit(solution)/shard_map/all_to_all | solution.py:18
  263.1 0.0 copy-start.3
  263.1 5.6 %fusion.5 = bf16[1,1280,640]{2,1,0:T(8,128)(2,1)} fusion(bf16[1024,1280]{1,0:T(8,128)(2,1)} %all-gather.4.cloned.1.call-done, bf16[1024,640]{1,0:T(8,128)(2,1)} %copy-done.5), kind=kOutput, calls=%fused_computation.12 | convolution fusion | flops 1678540800 | bytes 5570560 | tf_op jit(solution)/shard_map/dot_general | solution.py:54
  268.7 3.4 convolution_convert_fusion.4
  272.0 0.0 copy-done.3
  272.0 2.0 fusion.34
  274.1 5.6 %fusion.4 = bf16[2,256,1280]{2,1,0:T(8,128)(2,1)} fusion(f32[2,256,1280]{2,1,0:T(8,128)} %fusion.34, f32[2,256,128]{2,1,0:T(8,128)} %fusion.29, f32[2,256,128]{2,1,0:T(8,128)} %convolution_bitcast_fusion.2, bf16[1280,128]{1,0:T(8,128)(2,1)} %param.6, f32[2,256,128]{2,1,0:T(8,128)} %get-tuple-element.11, f32[2,256]{1,0:T(2,128)S(1)} %get-tuple-element.10), kind=kOutput, calls=%fused_computation.10 | convolution fusion | flops 169542272 | bytes 5048320 | tf_op jit(solution)/shard_map/its,ds->itd/dot_general | solution.py:74
  279.6 5.8 %all-to-all-done.4 = f32[64,20,128]{2,1,0:T(8,128)S(1)} async-done(((f32[64,20,128]{2,1,0:T(8,128)}), f32[64,20,128]{2,1,0:T(8,128)S(1)}, u32[]{:S(2)}, u32[]{:S(2)}) %all-to-all-start.4) | async-done | bytes 655392 | tf_op jit(solution)/shard_map/all_to_all | solution.py:18
  285.4 0.1 reduce_sum.49
  285.5 11.1 %psum.7 = f32[20,128]{1,0:T(8,128)S(1)} all-reduce(f32[20,128]{1,0:T(8,128)S(1)} %reduce_sum.49), channel_id=1, replica_groups=mesh['dp'=4,'wide'=16,'narrow'=4] {'dp'}, use_global_device_ids=true, to_apply=%region_9.0 | all-reduce | flops 2560 | bytes 20480 | tf_op jit(solution)/shard_map/psum | solution.py:79
  296.7 79.3 %all-gather = f32[64,20,128]{2,1,0:T(8,128)S(1)} all-gather(f32[1,20,128]{2,1,0:T(8,128)S(1)} %bitcast.56), channel_id=1, replica_groups=mesh['dp'=4,'wide'=16,'narrow'=4] {'wide','narrow'}, dimensions={0}, use_global_device_ids=true | all-gather | bytes 665600 | tf_op jit(solution)/shard_map/all_gather | solution.py:80
  376.0 0.9 reshape.53
  (2 shorter events, 0.0 us)
Async XLA Ops:
  7.2 74.3 %copy-start = (bf16[1,1280,640]{2,1,0:T(8,128)(2,1)S(1)}, bf16[1,1280,640]{2,1,0:T(8,128)(2,1)}, u32[]{:S(2)}) copy-start(bf16[1,1280,640]{2,1,0:T(8,128)(2,1)} %param.7) | copy-start | bytes 4915204
  7.2 74.3 %all-gather.4.cloned.1.call-start = ((), (), s32[]{:S(2)}) async-start(), calls=%async_computation.7 | async-start | bytes 3276800 | tf_op jit(solution)/shard_map/all_gather | solution.py:39
  46.7 75.1 %all-gather.6.cloned.1.call-start = ((), (), s32[]{:S(2)}) async-start(), calls=%async_computation.9 | async-start | bytes 3276800 | tf_op jit(solution)/shard_map/all_gather | solution.py:40
  78.1 91.8 %reduce-scatter.5.cloned.1.call-start = ((), (), s32[]{:S(2)}) async-start(), calls=%async_computation.10 | async-start | bytes 3276800 | tf_op jit(solution)/shard_map/reduce_scatter | solution.py:53
  91.6 41.5 %copy-start.4 = (bf16[1024,640]{1,0:T(8,128)(2,1)}, bf16[1024,640]{1,0:T(8,128)(2,1)S(1)}, u32[]{:S(2)}) copy-start(bf16[1024,640]{1,0:T(8,128)(2,1)S(1)} %get-tuple-element.5) | copy-start | bytes 3932164
  128.2 1.1 copy-start.5
  133.1 75.6 %reduce-scatter.3.cloned.1.call-start = ((), (), s32[]{:S(2)}) async-start(), calls=%async_computation.8 | async-start | bytes 3276800 | tf_op jit(solution)/shard_map/reduce_scatter | solution.py:47
  172.2 38.7 %all-to-all-start.3 = ((bf16[64,4,1280]{2,1,0:T(4,128)(2,1)}), bf16[64,4,1280]{2,1,0:T(4,128)(2,1)S(1)}, u32[]{:S(2)}, u32[]{:S(2)}) async-start(bf16[64,4,1280]{2,1,0:T(4,128)(2,1)} %reshape.49), calls=%async_computation.5 | async-start | bytes 1310720 | tf_op jit(solution)/shard_map/all_to_all | solution.py:18
  210.9 0.8 copy-start.2
  211.8 30.9 %all-to-all-start.1 = ((bf16[64,4,1280]{2,1,0:T(4,128)(2,1)}), bf16[64,4,1280]{2,1,0:T(4,128)(2,1)}, u32[]{:S(2)}, u32[]{:S(2)}) async-start(bf16[64,4,1280]{2,1,0:T(4,128)(2,1)} %reshape.45), calls=%async_computation.2 | async-start | bytes 1310720 | tf_op jit(solution)/shard_map/all_to_all | solution.py:18
  222.6 7.9 %copy-start.1 = (bf16[2,256,1280]{2,1,0:T(8,128)(2,1)S(1)}, bf16[2,256,1280]{2,1,0:T(8,128)(2,1)}, u32[]{:S(2)}) copy-start(bf16[2,256,1280]{2,1,0:T(8,128)(2,1)} %param.5) | copy-start | bytes 3932164
  256.9 28.5 %all-to-all-start.4 = ((f32[64,20,128]{2,1,0:T(8,128)}), f32[64,20,128]{2,1,0:T(8,128)S(1)}, u32[]{:S(2)}, u32[]{:S(2)}) async-start(f32[64,20,128]{2,1,0:T(8,128)} %reshape.51), calls=%async_computation.6 | async-start | bytes 1572864 | tf_op jit(solution)/shard_map/all_to_all | solution.py:18
  263.1 9.0 %copy-start.3 = (bf16[128,2,1280]{2,1,0:T(2,128)(2,1)S(1)}, bf16[128,2,1280]{2,1,0:T(2,128)(2,1)}, u32[]{:S(2)}) copy-start(bf16[128,2,1280]{2,1,0:T(2,128)(2,1)} %reshape.50) | copy-start | bytes 1966084
Sparse Core Ops, SparseCore 0:
  46.8 34.6 all-gather.3
  83.9 37.8 all-gather.5
  133.2 36.6 reduce-scatter.4
  172.3 36.2 reduce-scatter.2

commit v2 on v1

v2 whole, which is shorter than its diff:
```python
import functools

import jax
import jax.numpy as jnp
from jax import lax
from jax.experimental import pallas as pl
from jax.experimental.pallas import tpu as pltpu
from jax.sharding import PartitionSpec as P

MESH = pl.DeviceIdType.MESH
BF = jnp.bfloat16
F32 = jnp.float32
PH = 4
HALF = 640


def dot(a, b):
    return jnp.dot(a, b, preferred_element_type=F32)


def dot_nt(a, b):
    return lax.dot_general(a, b, (((1,), (1,)), ((), ())), preferred_element_type=F32)


def dot_tn(a, b):
    return lax.dot_general(a, b, (((0,), (0,)), ((), ())), preferred_element_type=F32)


def normal_cdf_pdf(x):
    z = jnp.abs(x) * 0.7071067811865476
    t = 1.0 / (1.0 + 0.5 * z)
    poly = 0.17087277
    for c in (
        -0.82215223,
        1.48851587,
        -1.13520398,
        0.27886807,
        -0.18628806,
        0.09678418,
        0.37409196,
        1.00002368,
        -1.26551223,
    ):
        poly = poly * t + c
    square = z * z
    tail = 0.5 * t * jnp.exp(poly - square)
    cdf = jnp.where(x < 0, tail, 1.0 - tail)
    pdf = 0.3989422804014327 * jnp.exp(-square)
    return cdf, pdf


def kernel(
    tok_h, rout_h, win_h, wout_h, cot_h,
    mixed_h, tg_h, rg_h, gi_h, go_h,
    tok, rout, win, wout, cot,
    perm, perm_t, disp, comb, stage, send, recv, gath, part, ring_a, ring_b, ring_c,
    pre, back_f, act, hid, ret, back, low, mixed, tgrad, ginv, goutv,
    rloc, ar0, half, ar1, ar2, one, fin,
    load_sem, out_sem, own_sem, a2a_send, a2a_recv, ag_send, ag_recv, rs_send, rs_recv,
    ret_send, ret_recv, ar_send, ar_recv,
):
    y = lax.axis_index("dp")
    wide = lax.axis_index("wide")
    narrow = lax.axis_index("narrow")
    me = wide * 4 + narrow
    z = lax.rem(wide, 8)
    x = (wide // 8) * 2 + narrow // 2
    core = lax.rem(narrow, 2)
    spot = y * 4 + x

    def plane(e):
        return {"wide": e // 4, "narrow": lax.rem(e, 4)}

    def chip(q):
        cx = lax.rem(q, 4)
        return {"dp": q // 4, "wide": (cx // 2) * 8 + z, "narrow": lax.rem(cx, 2) * 2 + core}

    up = {"dp": lax.rem(y + 1, 4)}
    down = {"dp": lax.rem(y + 3, 4)}

    loads = [
        pltpu.make_async_copy(a, b, load_sem.at[i])
        for i, (a, b) in enumerate(
            ((tok_h, tok), (rout_h, rout), (cot_h, cot), (win_h, win), (wout_h, wout))
        )
    ]
    for c in loads:
        c.start()

    barrier = pltpu.get_barrier_semaphore()

    def greet(k, _):
        pl.semaphore_signal(
            barrier, inc=1, device_id=plane(lax.rem(me + k, 64)), device_id_type=MESH
        )
        return _

    lax.fori_loop(1, 64, greet, 0)

    def greet_far(k, _):
        q = lax.rem(y + 1 + k // 4, 4) * 4 + lax.rem(k, 4)
        pl.semaphore_signal(barrier, inc=1, device_id=chip(q), device_id_type=MESH)
        return _

    lax.fori_loop(0, 12, greet_far, 0)

    def source(r):
        e16 = r // 16
        h = (r // 8) % 2
        c = (r // 4) % 2
        s = (r // 2) % 2
        return (h * 4 + c * 2 + r % 2) * 32 + e16 * 2 + s

    i0 = lax.broadcasted_iota(jnp.int32, (256, 256), 0)
    i1 = lax.broadcasted_iota(jnp.int32, (256, 256), 1)
    perm[...] = jnp.where(source(i0) == i1, 1.0, 0.0).astype(BF)
    perm_t[...] = jnp.where(source(i1) == i0, 1.0, 0.0).astype(BF)

    loads[0].wait()
    loads[1].wait()
    for i in range(2):
        rows = pl.ds(i * 256, 256)
        logits = dot(tok[rows, :], rout[...])
        d = jnp.exp(logits - jnp.max(logits, axis=0, keepdims=True))
        d = d / jnp.sum(d, axis=0, keepdims=True)
        c = jnp.exp(logits - jnp.max(logits, axis=1, keepdims=True))
        c = c / jnp.sum(c, axis=1, keepdims=True)
        disp[rows, :] = d
        comb[rows, :] = c
        if i == 0:
            loads[2].wait()
        for kind, (weight, values) in enumerate(((d, tok), (c, cot))):
            weight_t = weight.astype(BF).T
            for h in range(2):
                slots = dot(weight_t, values[rows, pl.ds(h * HALF, HALF)]).astype(BF)
                for g in range(4):
                    stage[g, pl.ds((h * 4 + kind * 2 + i) * 32, 32), :] = slots[
                        g * 32 : g * 32 + 32, :
                    ]
    for g in range(4):
        send[pl.ds(g * 256, 256), :] = dot(perm[...], stage[g]).astype(BF)

    pl.semaphore_wait(barrier, 75)

    own = pltpu.make_async_copy(
        send.at[pl.ds(pl.multiple_of(me * 16, 16), 16)], recv.at[pl.ds(0, 16)], own_sem.at[0]
    )
    own.start()
    for p in range(PH):

        def post(k, _, p=p):
            e = lax.rem(me + k, 64)
            pltpu.make_async_remote_copy(
                src_ref=send.at[pl.ds(pl.multiple_of(e * 16, 16), 16)],
                dst_ref=recv.at[pl.ds(pl.multiple_of(k * 16, 16), 16)],
                send_sem=a2a_send.at[0],
                recv_sem=a2a_recv.at[p],
                device_id=plane(e),
                device_id_type=MESH,
            ).start()
            return _

        lax.fori_loop(max(16 * p, 1), 16 * p + 16, post, 0)

    def wait_bytes(ref, sem):
        pltpu.make_async_copy(ref, ref, sem).wait()

    def remote(src, dst, s, r, to):
        return pltpu.make_async_remote_copy(
            src_ref=src, dst_ref=dst, send_sem=s, recv_sem=r, device_id=to, device_id_type=MESH
        )

    lo, hi = pl.ds(0, 2), pl.ds(2, 2)
    ag = {}
    rs = {}

    def stage_a(p):
        if p == 0:
            own.wait()
            wait_bytes(recv.at[pl.ds(16, 240)], a2a_recv.at[0])
        else:
            wait_bytes(recv.at[pl.ds(256 * p, 256)], a2a_recv.at[p])
        rows = dot(perm_t[...], recv[pl.ds(256 * p, 256), :]).astype(BF)
        gath[p, :, 0] = rows.reshape(4, 64, HALF)
        ag[p, 0] = remote(gath.at[p, :, 0], gath.at[p, :, 1], ag_send.at[p, 0], ag_recv.at[p, 0], up)
        ag[p, 1] = remote(gath.at[p, :, 0], gath.at[p, :, 3], ag_send.at[p, 1], ag_recv.at[p, 1], down)
        ag[p, 0].start()
        ag[p, 1].start()

    def stage_b(p):
        ag[p, 0].wait_recv()
        ag[p, 2] = remote(gath.at[p, lo, 1], gath.at[p, lo, 2], ag_send.at[p, 2], ag_recv.at[p, 2], up)
        ag[p, 2].start()
        ag[p, 1].wait_recv()
        ag[p, 3] = remote(gath.at[p, hi, 3], gath.at[p, hi, 2], ag_send.at[p, 3], ag_recv.at[p, 3], down)
        ag[p, 3].start()

    def stage_c(p):
        ag[p, 2].wait_recv()
        ag[p, 3].wait_recv()
        if p == 0:
            loads[3].wait()
            loads[4].wait()
        mine = pl.ds(256 * p, 256)

        def rows(q):
            return gath[p, q].reshape(256, HALF)

        pre[...] = dot(rows(0), win[pl.ds(0, HALF), :]) + dot(rows(2), win[pl.ds(HALF, HALF), :])
        back_f[...] = dot_nt(rows(1), wout[:, pl.ds(0, HALF)]) + dot_nt(
            rows(3), wout[:, pl.ds(HALF, HALF)]
        )

        def nonlinear(j, _):
            r = pl.ds(pl.multiple_of(j * 16, 16), 16)
            v = pre[r, :]
            cdf, pdf = normal_cdf_pdf(v)
            to = pl.ds(pl.multiple_of(256 * p + j * 16, 16), 16)
            act[to, :] = (v * cdf).astype(BF)
            hid[to, :] = (back_f[r, :] * (cdf + v * pdf)).astype(BF)
            return _

        lax.fori_loop(0, 16, nonlinear, 0)
        for h in range(2):
            cols = pl.ds(h * HALF, HALF)
            part[p, 2 * h] = dot(act[mine, :], wout[:, cols]).astype(BF).reshape(4, 64, HALF)
            part[p, 2 * h + 1] = dot_nt(hid[mine, :], win[cols, :]).astype(BF).reshape(4, 64, HALF)
        rs[p, 0] = remote(part.at[p, lo, 2], ring_a.at[p, 0], rs_send.at[p, 0], rs_recv.at[p, 0], up)
        rs[p, 1] = remote(part.at[p, hi, 2], ring_a.at[p, 1], rs_send.at[p, 1], rs_recv.at[p, 1], down)
        rs[p, 2] = remote(part.at[p, hi, 3], ring_b.at[p, hi], rs_send.at[p, 2], rs_recv.at[p, 2], up)
        rs[p, 3] = remote(part.at[p, lo, 1], ring_c.at[p, lo], rs_send.at[p, 3], rs_recv.at[p, 3], down)
        for j in range(4):
            rs[p, j].start()

    def stage_d(p):
        rs[p, 0].wait_recv()
        part[p, lo, 3] = (part[p, lo, 3].astype(F32) + ring_a[p, 0].astype(F32)).astype(BF)
        rs[p, 4] = remote(part.at[p, lo, 3], ring_b.at[p, lo], rs_send.at[p, 4], rs_recv.at[p, 4], up)
        rs[p, 4].start()
        rs[p, 1].wait_recv()
        part[p, hi, 1] = (part[p, hi, 1].astype(F32) + ring_a[p, 1].astype(F32)).astype(BF)
        rs[p, 5] = remote(part.at[p, hi, 1], ring_c.at[p, hi], rs_send.at[p, 5], rs_recv.at[p, 5], down)
        rs[p, 5].start()

    def stage_e(p):
        for j in range(2, 6):
            rs[p, j].wait_recv()
        total = part[p, :, 0].astype(F32) + ring_b[p].astype(F32) + ring_c[p].astype(F32)
        ret[pl.ds(256 * p, 256), :] = dot(perm[...], total.astype(BF).reshape(256, HALF)).astype(BF)

        def post(k, _):
            pltpu.make_async_remote_copy(
                src_ref=ret.at[pl.ds(pl.multiple_of(k * 16, 16), 16)],
                dst_ref=back.at[pl.ds(pl.multiple_of(me * 16, 16), 16)],
                send_sem=ret_send.at[0],
                recv_sem=ret_recv.at[0],
                device_id=plane(lax.rem(me + 64 - k, 64)),
                device_id_type=MESH,
            ).start()
            return _

        lax.fori_loop(max(16 * p, 1), 16 * p + 16, post, 0)
        if p == 0:
            pltpu.make_async_copy(
                ret.at[pl.ds(0, 16)], back.at[pl.ds(pl.multiple_of(me * 16, 16), 16)], own_sem.at[1]
            ).start()

    def grad_first(h):
        total = None
        for p in range(PH):
            term = dot_tn(gath[p, 2 * h].reshape(256, HALF), hid[pl.ds(256 * p, 256), :])
            total = term if total is None else total + term
        ginv[pl.ds(h * HALF, HALF), :] = total.astype(BF)

    def grad_second(h):
        total = None
        for p in range(PH):
            term = dot_tn(act[pl.ds(256 * p, 256), :], gath[p, 2 * h + 1].reshape(256, HALF))
            total = term if total is None else total + term
        goutv[:, pl.ds(h * HALF, HALF)] = total.astype(BF)

    stage_a(0)
    stage_a(1)
    stage_b(0)
    stage_a(2)
    stage_b(1)
    stage_c(0)
    stage_a(3)
    stage_b(2)
    stage_c(1)
    stage_d(0)
    stage_b(3)
    stage_c(2)
    stage_d(1)
    stage_e(0)
    stage_c(3)
    stage_d(2)
    stage_e(1)
    grad_first(0)
    grad_first(1)
    out_gi = pltpu.make_async_copy(ginv, gi_h, out_sem.at[0])
    out_gi.start()
    stage_d(3)
    stage_e(2)
    grad_second(0)
    grad_second(1)
    out_go = pltpu.make_async_copy(goutv, go_h, out_sem.at[1])
    out_go.start()
    stage_e(3)

    pltpu.make_async_copy(
        ret.at[pl.ds(0, 16)], back.at[pl.ds(pl.multiple_of(me * 16, 16), 16)], own_sem.at[1]
    ).wait()
    wait_bytes(back.at[pl.ds(0, 63 * 16)], ret_recv.at[0])
    for g in range(4):
        rows = dot(perm_t[...], back[pl.ds(g * 256, 256), :]).astype(BF)
        for j in range(8):
            low[j, pl.ds(g * 32, 32), :] = rows[j * 32 : j * 32 + 32, :]
    logit = []
    turned = []
    for i in range(2):
        rows = pl.ds(i * 256, 256)
        h0, h1 = pl.ds(0, HALF), pl.ds(HALF, HALF)
        left = dot_nt(cot[rows, h0], low[i]) + dot_nt(cot[rows, h1], low[4 + i])
        right = dot_nt(tok[rows, h0], low[2 + i]) + dot_nt(tok[rows, h1], low[6 + i])
        c, d = comb[rows, :], disp[rows, :]
        g = c * (left - jnp.sum(c * left, axis=1, keepdims=True))
        g = g + d * (right - jnp.sum(d * right, axis=0, keepdims=True))
        logit.append(g.astype(BF))
        turned.append(g.astype(BF).T)
    for j in range(5):
        cols = pl.ds(j * 256, 256)
        term = dot(turned[0], tok[pl.ds(0, 256), cols]) + dot(turned[1], tok[pl.ds(256, 256), cols])
        rloc[cols, :] = term.T

    sibling = {"narrow": narrow + 1 - 2 * core}
    keep = pl.ds(pl.multiple_of(core * HALF, HALF), HALF)
    give = pl.ds(pl.multiple_of((1 - core) * HALF, HALF), HALF)
    first = remote(rloc.at[give], ar0, ar_send.at[0], ar_recv.at[0], sibling)
    first.start()

    def image_out(i):
        rows = pl.ds(i * 256, 256)
        dl = disp[rows, :].astype(BF)
        cl = comb[rows, :].astype(BF)
        for h in range(2):
            cols = pl.ds(h * HALF, HALF)
            mixed[rows, cols] = dot(cl, low[h * 4 + i]).astype(BF)
            tgrad[rows, cols] = (
                dot(dl, low[h * 4 + 2 + i]) + dot_nt(logit[i], rout[cols, :])
            ).astype(BF)

    first.wait_recv()
    half[...] = rloc[keep, :] + ar0[...]

    def scatter(j, _):
        q = lax.rem(spot + j, 16)
        remote(
            half.at[pl.ds(pl.multiple_of(q * 40, 8), 40)], ar1.at[j],
            ar_send.at[1], ar_recv.at[1], chip(q),
        ).start()
        return _

    lax.fori_loop(1, 16, scatter, 0)
    image_out(0)
    wait_bytes(ar1.at[pl.ds(1, 15)], ar_recv.at[1])
    total = half[pl.ds(pl.multiple_of(spot * 40, 8), 40), :]
    for j in range(1, 16):
        total = total + ar1[j]
    one[...] = total
    ar2[z] = total

    def across(j, _):
        to = (wide // 8) * 8 + lax.rem(z + j, 8)
        remote(one, ar2.at[z], ar_send.at[2], ar_recv.at[2], {"wide": to}).start()
        return _

    lax.fori_loop(1, 8, across, 0)
    image_out(1)
    out_mixed = pltpu.make_async_copy(mixed, mixed_h, out_sem.at[2])
    out_mixed.start()
    out_tg = pltpu.make_async_copy(tgrad, tg_h, out_sem.at[3])
    out_tg.start()
    wait_bytes(ar2.at[pl.ds(0, 7)], ar_recv.at[2])
    total = ar2[0]
    for j in range(1, 8):
        total = total + ar2[j]
    place = pl.ds(pl.multiple_of(core * HALF + spot * 40, 8), 40)
    fin[place, :] = total

    def spread(j, _):
        q = lax.rem(spot + j, 16)
        remote(fin.at[place], fin.at[place], ar_send.at[3], ar_recv.at[3], chip(q)).start()
        return _

    lax.fori_loop(1, 16, spread, 0)
    wait_bytes(ar1.at[pl.ds(1, 15)], ar_recv.at[3])
    last = remote(fin.at[keep], fin.at[keep], ar_send.at[4], ar_recv.at[4], sibling)
    last.start()
    last.wait_recv()
    out_rg = pltpu.make_async_copy(fin, rg_h, out_sem.at[4])
    out_rg.start()

    wait_bytes(recv.at[pl.ds(0, 63 * 16)], a2a_send.at[0])
    wait_bytes(recv.at[pl.ds(0, 63 * 16)], ret_send.at[0])
    for c in list(ag.values()) + list(rs.values()):
        c.wait_send()
    first.wait_send()
    last.wait_send()
    wait_bytes(ar1.at[pl.ds(1, 15)], ar_send.at[1])
    wait_bytes(ar2.at[pl.ds(0, 7)], ar_send.at[2])
    wait_bytes(ar1.at[pl.ds(1, 15)], ar_send.at[3])
    for c in (out_gi, out_go, out_mixed, out_tg, out_rg):
        c.wait()


def local(tokens, router, expert_in, expert_out, cotangent):
    images, length, width = tokens.shape
    slots = router.shape[1]
    hidden = expert_in.shape[2]
    rows = images * length
    vm = pltpu.VMEM
    dma = pltpu.SemaphoreType.DMA
    anywhere = pl.BlockSpec(memory_space=pl.ANY)
    out = pl.pallas_call(
        kernel,
        out_shape=(
            jax.ShapeDtypeStruct((rows, width), BF),
            jax.ShapeDtypeStruct((rows, width), BF),
            jax.ShapeDtypeStruct((width, slots), F32),
            jax.ShapeDtypeStruct((width, hidden), BF),
            jax.ShapeDtypeStruct((hidden, width), BF),
        ),
        in_specs=[anywhere] * 5,
        out_specs=[anywhere] * 5,
        scratch_shapes=[
            vm((rows, width), BF), vm((width, slots), BF), vm((width, hidden), BF),
            vm((hidden, width), BF), vm((rows, width), BF),
            vm((256, 256), BF), vm((256, 256), BF),
            vm((rows, slots), F32), vm((rows, slots), F32),
            vm((4, 256, HALF), BF), vm((1024, HALF), BF), vm((1024, HALF), BF),
            vm((PH, 4, 4, 64, HALF), BF), vm((PH, 4, 4, 64, HALF), BF),
            vm((PH, 2, 2, 64, HALF), BF),
            vm((PH, 4, 64, HALF), BF), vm((PH, 4, 64, HALF), BF),
            vm((256, hidden), F32), vm((256, hidden), F32),
            vm((1024, hidden), BF), vm((1024, hidden), BF),
            vm((1024, HALF), BF), vm((1024, HALF), BF),
            vm((8, 128, HALF), BF),
            vm((rows, width), BF), vm((rows, width), BF),
            vm((width, hidden), BF), vm((hidden, width), BF),
            vm((width, slots), F32), vm((HALF, slots), F32), vm((HALF, slots), F32),
            vm((16, 40, slots), F32), vm((8, 40, slots), F32), vm((40, slots), F32),
            vm((width, slots), F32),
            dma((5,)), dma((5,)), dma((2,)), dma((1,)), dma((PH,)),
            dma((PH, 4)), dma((PH, 4)), dma((PH, 6)), dma((PH, 6)),
            dma((1,)), dma((1,)), dma((5,)), dma((5,)),
        ],
        compiler_params=pltpu.CompilerParams(
            collective_id=0, has_side_effects=True, vmem_limit_bytes=60 * 1024 * 1024
        ),
        cost_estimate=pl.CostEstimate(
            flops=12 * 10**9, bytes_accessed=12 * 10**6, transcendentals=2 * 10**6
        ),
    )(
        tokens.reshape(rows, width), router, expert_in[0], expert_out[0],
        cotangent.reshape(rows, width),
    )
    mixed, token_grad, router_grad, grad_in, grad_out = out
    return (
        mixed.reshape(images, length, width),
        token_grad.reshape(images, length, width),
        router_grad,
        grad_in[None],
        grad_out[None],
    )


def solution(mesh):
    in_specs = (
        P(("dp", "wide", "narrow"), None, None),
        P(),
        P(("wide", "narrow"), None, "dp"),
        P(("wide", "narrow"), "dp", None),
        P(("dp", "wide", "narrow"), None, None),
    )
    out_specs = (
        P(("dp", "wide", "narrow"), None, None),
        P(("dp", "wide", "narrow"), None, None),
        P(),
        P(("wide", "narrow"), None, "dp"),
        P(("wide", "narrow"), "dp", None),
    )
    return jax.shard_map(local, mesh=mesh, in_specs=in_specs, out_specs=out_specs, check_vma=False)
```

time: 384 us -> 168 us (0.44)
  Pallas kernels: 0 us -> 159 us
  blocking collectives: 149 us -> 0 us
  waiting for transfers between devices: 107 us -> 0 us
  matrix products: 63.2 us -> 0 us
  starting transfers between devices: 27.8 us -> 0 us
  between operations: 13.9 us -> 0.65 us
  local copies, waits for them, and re-layouts: 18.7 us -> 8.12 us
    pallas_call x0 -> x1, Pallas kernels: none -> 159 us  [local(): pl.pallas_call(kernel, out_shape=(jax.ShapeDtypeStruct((rows, width), BF)...]
    all_gather x1 -> x0, blocking collectives: 79.3 us -> none  [local(): router_grad = lax.all_gather(share, PLANE, axis=0, tiled=True)]
    dot_general x15 -> x0, matrix products: 63.2 us -> none  [the longest x2 15.3 us: dot(): return jnp.dot(a, b, preferred_element_type=jnp.float32)]
    all_to_all x2 -> x0, blocking collectives: 59 us -> none  [exchange(): return lax.all_to_all(x, PLANE, split_axis=0, concat_axis=0, tiled=True)]
    reduce_scatter x2 -> x0, waiting for transfers between devices: 57.5 us -> none  [the longest x1 31.6 us: local(): lax.psum_scatter(grad_part, 'dp', scatter_dimension=0, tiled=True)]
    all_gather x2 -> x0, waiting for transfers between devices: 33.3 us -> none  [the longest x1 30.2 us: local(): lax.all_gather(exchange(slot_cot.reshape(shape)).reshape(-1, width), 'dp'...]
    all_to_all x3 -> x0, starting transfers between devices: 27.5 us -> none  [exchange(): return lax.all_to_all(x, PLANE, split_axis=0, concat_axis=0, tiled=True)]
    all_to_all x3 -> x0, waiting for transfers between devices: 15.7 us -> none  [exchange(): return lax.all_to_all(x, PLANE, split_axis=0, concat_axis=0, tiled=True)]
  transfers between devices with their start and end apart: 7 -> 0, of which waited for: 6 -> 0; matrix products, arithmetic and copies ran while one was open for 14% -> 0% of each run, Pallas kernels for 0% -> 0%
where the time goes in v2:
time: 168 us
  Pallas kernels  159 us (95%)
  local copies, waits for them, and re-layouts  8.12 us (5%)
    pallas_call x1, Pallas kernels, local(): pl.pallas_call(kernel, out_shape=(jax.ShapeDtypeStruct((rows, width), BF)...  159 us
    unnamed x13, local copies, waits for them, and re-layouts  8.12 us

profile of v2, /device:TPU:1, one launch (start us, length us, event | category | flops | bytes accessed | tf_op | source)
XLA Modules:
  0.0 168.2 jit_solution(7383202578743298233)
XLA Ops:
  0.6 159.4 %shard_map.92 = (bf16[512,1280]{1,0:T(8,128)(2,1)}, bf16[512,1280]{1,0:T(8,128)(2,1)}, f32[1280,128]{1,0:T(8,128)}, bf16[1280,640]{1,0:T(8,128)(2,1)}, bf16[640,1280]{1,0:T(8,128)(2,1)}) custom-call(bf16[512,1280]{1,0:T(8,128)(2,1)} %bitcast.14, bf16[1280,128]{1,0:T(8,128)(2,1)} %rout_h.1, bf16[1280,640]{1,0:T(8,128)(2,1)} %bitcast.12, ...), custom_call_target="tpu_custom_call" | custom-call | flops 12000000000 | bytes 12000000 | tf_op jit(solution)/shard_map/pallas_call | solution.py:425
  160.1 0.0 copy-start.2
  160.1 2.6 %copy.15 = bf16[2,256,1280]{2,1,0:T(8,128)(2,1)} copy(bf16[2,256,1280]{2,1,0:T(8,128)(2,1)} %bitcast.11) | data formatting | bytes 2621440
  162.6 0.0 copy-done.2
  162.7 0.0 copy-start.3
  162.7 0.0 copy-start.1
  162.7 1.1 copy.16
  163.7 0.5 copy-done.3
  164.2 0.8 copy.17
  165.0 0.0 copy-done.1
  165.0 0.0 copy-start
  165.0 1.2 copy.18
  166.2 0.9 copy-done
  167.1 1.2 copy.19
Async XLA Ops:
  160.1 2.6 %copy-start.2 = (bf16[512,1280]{1,0:T(8,128)(2,1)S(1)}, bf16[512,1280]{1,0:T(8,128)(2,1)}, u32[]{:S(2)}) copy-start(bf16[512,1280]{1,0:T(8,128)(2,1)} %get-tuple-element.11) | copy-start | bytes 3932164
  162.7 1.5 copy-start.3
  162.7 2.4 %copy-start.1 = (bf16[1280,640]{1,0:T(8,128)(2,1)S(1)}, bf16[1280,640]{1,0:T(8,128)(2,1)}, u32[]{:S(2)}) copy-start(bf16[1280,640]{1,0:T(8,128)(2,1)} %get-tuple-element.13) | copy-start | bytes 4915204
  165.0 2.0 %copy-start = (bf16[640,1280]{1,0:T(8,128)(2,1)S(1)}, bf16[640,1280]{1,0:T(8,128)(2,1)}, u32[]{:S(2)}) copy-start(bf16[640,1280]{1,0:T(8,128)(2,1)} %get-tuple-element.14) | copy-start | bytes 4915204

commit v3 on v2

v3 whole, which is shorter than its diff:
```python
import functools

import jax
import jax.numpy as jnp
from jax import lax
from jax.experimental import pallas as pl
from jax.experimental.pallas import tpu as pltpu
from jax.sharding import PartitionSpec as P

MESH = pl.DeviceIdType.MESH
BF = jnp.bfloat16
F32 = jnp.float32
PH = 8
MSG = 64 // PH
ROWS = 16 * MSG
EACH = ROWS // 4
CHAINS = ((0, 24), (24, 16))
HALF = 640


def dot(a, b):
    return jnp.dot(a, b, preferred_element_type=F32)


def dot_nt(a, b):
    return lax.dot_general(a, b, (((1,), (1,)), ((), ())), preferred_element_type=F32)


def dot_tn(a, b):
    return lax.dot_general(a, b, (((0,), (0,)), ((), ())), preferred_element_type=F32)


def normal_cdf_pdf(x):
    z = jnp.abs(x) * 0.7071067811865476
    t = 1.0 / (1.0 + 0.5 * z)
    poly = 0.17087277
    for c in (
        -0.82215223,
        1.48851587,
        -1.13520398,
        0.27886807,
        -0.18628806,
        0.09678418,
        0.37409196,
        1.00002368,
        -1.26551223,
    ):
        poly = poly * t + c
    square = z * z
    tail = 0.5 * t * jnp.exp(poly - square)
    cdf = jnp.where(x < 0, tail, 1.0 - tail)
    pdf = 0.3989422804014327 * jnp.exp(-square)
    return cdf, pdf


def kernel(
    tok_h, rout_h, win_h, wout_h, cot_h,
    mixed, tgrad, fin, ginv, goutv,
    tok, rout, win, wout, cot,
    perm, perm_t, disp, comb, stage, send, recv, gath, part, ring_a, ring_b, ring_c,
    pre, back_f, act, hid, ret, back, low,
    give_v, keep_v, ar0_a, ar0_b, half_a, half_b, ar1_a, ar1_b, one_a, one_b, ar2_a, ar2_b,
    load_sem, own_sem, a2a_send, a2a_recv, ag_send, ag_recv, rs_send, rs_recv,
    ret_send, ret_recv, ar_send, ar_recv,
):
    y = lax.axis_index("dp")
    wide = lax.axis_index("wide")
    narrow = lax.axis_index("narrow")
    me = wide * 4 + narrow
    z = lax.rem(wide, 8)
    x = (wide // 8) * 2 + narrow // 2
    core = lax.rem(narrow, 2)
    spot = y * 4 + x

    def plane(e):
        return {"wide": e // 4, "narrow": lax.rem(e, 4)}

    def place_of(k, sign):
        j = k % 8
        dz = (j % 2) * ((j + 1) // 2) + (1 - j % 2) * (8 - j // 2)
        px = (x + sign * (k // 16) + 4) % 4
        pz = (z + sign * dz + 8) % 8
        pc = (core + k // 8) % 2
        return (px // 2) * 8 + pz, (px % 2) * 2 + pc

    def chip(q):
        cx = lax.rem(q, 4)
        return {"dp": q // 4, "wide": (cx // 2) * 8 + z, "narrow": lax.rem(cx, 2) * 2 + core}

    up = {"dp": lax.rem(y + 1, 4)}
    down = {"dp": lax.rem(y + 3, 4)}

    loads = [
        pltpu.make_async_copy(a, b, load_sem.at[i])
        for i, (a, b) in enumerate(
            ((tok_h, tok), (rout_h, rout), (cot_h, cot), (win_h, win), (wout_h, wout))
        )
    ]
    for c in loads:
        c.start()

    barrier = pltpu.get_barrier_semaphore()

    def greet(k, _):
        pl.semaphore_signal(
            barrier, inc=1, device_id=plane(lax.rem(me + k, 64)), device_id_type=MESH
        )
        return _

    lax.fori_loop(1, 64, greet, 0)

    def greet_far(k, _):
        q = lax.rem(y + 1 + k // 4, 4) * 4 + lax.rem(k, 4)
        pl.semaphore_signal(barrier, inc=1, device_id=chip(q), device_id_type=MESH)
        return _

    lax.fori_loop(0, 12, greet_far, 0)

    def source(r):
        e = r // 16
        h = (r // 8) % 2
        c = (r // 4) % 2
        s = (r // 2) % 2
        return (h * 4 + c * 2 + r % 2) * EACH // 2 + e * 2 + s

    i0 = lax.broadcasted_iota(jnp.int32, (ROWS, ROWS), 0)
    i1 = lax.broadcasted_iota(jnp.int32, (ROWS, ROWS), 1)
    perm[...] = jnp.where(source(i0) == i1, 1.0, 0.0).astype(BF)
    perm_t[...] = jnp.where(source(i1) == i0, 1.0, 0.0).astype(BF)

    loads[0].wait()
    loads[1].wait()
    for i in range(2):
        rows = pl.ds(i * 256, 256)
        logits = dot(tok[rows, :], rout[...])
        d = jnp.exp(logits - jnp.max(logits, axis=0, keepdims=True))
        d = d / jnp.sum(d, axis=0, keepdims=True)
        c = jnp.exp(logits - jnp.max(logits, axis=1, keepdims=True))
        c = c / jnp.sum(c, axis=1, keepdims=True)
        disp[rows, :] = d
        comb[rows, :] = c
        if i == 0:
            loads[2].wait()
        for kind, (weight, values) in enumerate(((d, tok), (c, cot))):
            weight_t = weight.astype(BF).T
            for h in range(2):
                slots = dot(weight_t, values[rows, pl.ds(h * HALF, HALF)]).astype(BF)
                for g in range(PH):
                    stage[g, pl.ds((h * 4 + kind * 2 + i) * EACH // 2, EACH // 2), :] = slots[
                        g * EACH // 2 : (g + 1) * EACH // 2, :
                    ]
    for g in range(PH):
        send[pl.ds(g * ROWS, ROWS), :] = dot(perm[...], stage[g]).astype(BF)

    pl.semaphore_wait(barrier, 75)

    own = pltpu.make_async_copy(
        send.at[pl.ds(pl.multiple_of(me * 16, 16), 16)], recv.at[pl.ds(0, 16)], own_sem.at[0]
    )
    own.start()
    for p in range(PH):

        def post(k, _, p=p):
            w, n = place_of(k, 1)
            pltpu.make_async_remote_copy(
                src_ref=send.at[pl.ds(pl.multiple_of((w * 4 + n) * 16, 16), 16)],
                dst_ref=recv.at[pl.ds(pl.multiple_of(k * 16, 16), 16)],
                send_sem=a2a_send.at[0],
                recv_sem=a2a_recv.at[p],
                device_id={"wide": w, "narrow": n},
                device_id_type=MESH,
            ).start()
            return _

        lax.fori_loop(max(MSG * p, 1), MSG * p + MSG, post, 0)

    def wait_bytes(ref, sem):
        pltpu.make_async_copy(ref, ref, sem).wait()

    def remote(src, dst, s, r, to):
        return pltpu.make_async_remote_copy(
            src_ref=src, dst_ref=dst, send_sem=s, recv_sem=r, device_id=to, device_id_type=MESH
        )

    lo, hi = pl.ds(0, 2), pl.ds(2, 2)
    ag = {}
    rs = {}

    def stage_a(p):
        if p == 0:
            own.wait()
            wait_bytes(recv.at[pl.ds(16, ROWS - 16)], a2a_recv.at[0])
        else:
            wait_bytes(recv.at[pl.ds(ROWS * p, ROWS)], a2a_recv.at[p])
        rows = dot(perm_t[...], recv[pl.ds(ROWS * p, ROWS), :]).astype(BF)
        gath[p, :, 0] = rows.reshape(4, EACH, HALF)
        ag[p, 0] = remote(gath.at[p, :, 0], gath.at[p, :, 1], ag_send.at[p, 0], ag_recv.at[p, 0], up)
        ag[p, 1] = remote(gath.at[p, :, 0], gath.at[p, :, 3], ag_send.at[p, 1], ag_recv.at[p, 1], down)
        ag[p, 0].start()
        ag[p, 1].start()

    def stage_b(p):
        ag[p, 0].wait_recv()
        ag[p, 2] = remote(gath.at[p, lo, 1], gath.at[p, lo, 2], ag_send.at[p, 2], ag_recv.at[p, 2], up)
        ag[p, 2].start()
        ag[p, 1].wait_recv()
        ag[p, 3] = remote(gath.at[p, hi, 3], gath.at[p, hi, 2], ag_send.at[p, 3], ag_recv.at[p, 3], down)
        ag[p, 3].start()

    def stage_c(p):
        ag[p, 2].wait_recv()
        ag[p, 3].wait_recv()
        if p == 0:
            loads[3].wait()
            loads[4].wait()
        mine = pl.ds(4 * EACH * p, 4 * EACH)

        def rows(q):
            return gath[p, q].reshape(4 * EACH, HALF)

        pre[...] = dot(rows(0), win[pl.ds(0, HALF), :]) + dot(rows(2), win[pl.ds(HALF, HALF), :])
        back_f[...] = dot_nt(rows(1), wout[:, pl.ds(0, HALF)]) + dot_nt(
            rows(3), wout[:, pl.ds(HALF, HALF)]
        )

        def nonlinear(j, _):
            r = pl.ds(pl.multiple_of(j * 16, 16), 16)
            v = pre[r, :]
            cdf, pdf = normal_cdf_pdf(v)
            to = pl.ds(pl.multiple_of(4 * EACH * p + j * 16, 16), 16)
            act[to, :] = (v * cdf).astype(BF)
            hid[to, :] = (back_f[r, :] * (cdf + v * pdf)).astype(BF)
            return _

        lax.fori_loop(0, EACH // 4, nonlinear, 0)
        for h in range(2):
            cols = pl.ds(h * HALF, HALF)
            part[p, 2 * h] = dot(act[mine, :], wout[:, cols]).astype(BF).reshape(4, EACH, HALF)
            part[p, 2 * h + 1] = dot_nt(hid[mine, :], win[cols, :]).astype(BF).reshape(4, EACH, HALF)
        rs[p, 0] = remote(part.at[p, lo, 2], ring_a.at[p, 0], rs_send.at[p, 0], rs_recv.at[p, 0], up)
        rs[p, 1] = remote(part.at[p, hi, 2], ring_a.at[p, 1], rs_send.at[p, 1], rs_recv.at[p, 1], down)
        rs[p, 2] = remote(part.at[p, hi, 3], ring_b.at[p, hi], rs_send.at[p, 2], rs_recv.at[p, 2], up)
        rs[p, 3] = remote(part.at[p, lo, 1], ring_c.at[p, lo], rs_send.at[p, 3], rs_recv.at[p, 3], down)
        for j in range(4):
            rs[p, j].start()

    def stage_d(p):
        rs[p, 0].wait_recv()
        part[p, lo, 3] = (part[p, lo, 3].astype(F32) + ring_a[p, 0].astype(F32)).astype(BF)
        rs[p, 4] = remote(part.at[p, lo, 3], ring_b.at[p, lo], rs_send.at[p, 4], rs_recv.at[p, 4], up)
        rs[p, 4].start()
        rs[p, 1].wait_recv()
        part[p, hi, 1] = (part[p, hi, 1].astype(F32) + ring_a[p, 1].astype(F32)).astype(BF)
        rs[p, 5] = remote(part.at[p, hi, 1], ring_c.at[p, hi], rs_send.at[p, 5], rs_recv.at[p, 5], down)
        rs[p, 5].start()

    def stage_e(p):
        for j in range(2, 6):
            rs[p, j].wait_recv()
        total = part[p, :, 0].astype(F32) + ring_b[p].astype(F32) + ring_c[p].astype(F32)
        ret[pl.ds(ROWS * p, ROWS), :] = dot(perm[...], total.astype(BF).reshape(ROWS, HALF)).astype(BF)

        def post(k, _):
            w, n = place_of(k, -1)
            pltpu.make_async_remote_copy(
                src_ref=ret.at[pl.ds(pl.multiple_of(k * 16, 16), 16)],
                dst_ref=back.at[pl.ds(pl.multiple_of(me * 16, 16), 16)],
                send_sem=ret_send.at[0],
                recv_sem=ret_recv.at[0],
                device_id={"wide": w, "narrow": n},
                device_id_type=MESH,
            ).start()
            return _

        lax.fori_loop(max(MSG * p, 1), MSG * p + MSG, post, 0)
        if p == 0:
            pltpu.make_async_copy(
                ret.at[pl.ds(0, 16)], back.at[pl.ds(pl.multiple_of(me * 16, 16), 16)], own_sem.at[1]
            ).start()

    def grad_first(h):
        total = None
        for p in range(PH):
            term = dot_tn(
                gath[p, 2 * h].reshape(4 * EACH, HALF), hid[pl.ds(4 * EACH * p, 4 * EACH), :]
            )
            total = term if total is None else total + term
        ginv[pl.ds(h * HALF, HALF), :] = total.astype(BF)

    def grad_second(h):
        total = None
        for p in range(PH):
            term = dot_tn(
                act[pl.ds(4 * EACH * p, 4 * EACH), :], gath[p, 2 * h + 1].reshape(4 * EACH, HALF)
            )
            total = term if total is None else total + term
        goutv[:, pl.ds(h * HALF, HALF)] = total.astype(BF)

    for t in range(PH + 4):
        if t < PH:
            stage_a(t)
        if 0 <= t - 1 < PH:
            stage_b(t - 1)
        if 0 <= t - 2 < PH:
            stage_c(t - 2)
        if 0 <= t - 3 < PH:
            stage_d(t - 3)
        if t == PH + 2:
            grad_first(0)
            grad_first(1)
        if 0 <= t - 4 < PH:
            stage_e(t - 4)
    grad_second(0)
    grad_second(1)

    pltpu.make_async_copy(
        ret.at[pl.ds(0, 16)], back.at[pl.ds(pl.multiple_of(me * 16, 16), 16)], own_sem.at[1]
    ).wait()
    wait_bytes(back.at[pl.ds(0, 63 * 16)], ret_recv.at[0])
    for g in range(PH):
        rows = dot(perm_t[...], back[pl.ds(g * ROWS, ROWS), :]).astype(BF)
        for j in range(8):
            low[j, pl.ds(g * EACH // 2, EACH // 2), :] = rows[j * EACH // 2 : (j + 1) * EACH // 2, :]
    logit = []
    turned = []
    for i in range(2):
        rows = pl.ds(i * 256, 256)
        h0, h1 = pl.ds(0, HALF), pl.ds(HALF, HALF)
        left = dot_nt(cot[rows, h0], low[i]) + dot_nt(cot[rows, h1], low[4 + i])
        right = dot_nt(tok[rows, h0], low[2 + i]) + dot_nt(tok[rows, h1], low[6 + i])
        c, d = comb[rows, :], disp[rows, :]
        g = c * (left - jnp.sum(c * left, axis=1, keepdims=True))
        g = g + d * (right - jnp.sum(d * right, axis=0, keepdims=True))
        logit.append(g.astype(BF))
        turned.append(g.astype(BF).T)

    def router_half(which):
        cols = pl.ds(pl.multiple_of(which * HALF, HALF), HALF)
        term = dot(turned[0], tok[pl.ds(0, 256), cols]) + dot(turned[1], tok[pl.ds(256, 256), cols])
        return term.T.reshape(16, 40, 128)

    sibling = {"narrow": narrow + 1 - 2 * core}
    chains = [
        (c, pl.ds(off, n), n, *refs)
        for c, ((off, n), refs) in enumerate(
            zip(
                CHAINS,
                ((ar0_a, half_a, ar1_a, one_a, ar2_a), (ar0_b, half_b, ar1_b, one_b, ar2_b)),
            )
        )
    ]
    give_v[...] = router_half(1 - core)
    first = []
    for c, span, n, ar0, half, ar1, one, ar2 in chains:
        first.append(
            remote(give_v.at[:, span], ar0, ar_send.at[0, c], ar_recv.at[0, c], sibling)
        )
        first[-1].start()
    keep_v[...] = router_half(core)

    def image_out(i):
        rows = pl.ds(i * 256, 256)
        dl = disp[rows, :].astype(BF)
        cl = comb[rows, :].astype(BF)
        for h in range(2):
            cols = pl.ds(h * HALF, HALF)
            mixed[rows, cols] = dot(cl, low[h * 4 + i]).astype(BF)
            tgrad[rows, cols] = (
                dot(dl, low[h * 4 + 2 + i]) + dot_nt(logit[i], rout[cols, :])
            ).astype(BF)

    for c, span, n, ar0, half, ar1, one, ar2 in chains:
        first[c].wait_recv()
        half[...] = keep_v[:, span, :] + ar0[...]

        def scatter(j, _, c=c, half=half, ar1=ar1):
            q = lax.rem(spot + j, 16)
            remote(half.at[q], ar1.at[j], ar_send.at[1, c], ar_recv.at[1, c], chip(q)).start()
            return _

        lax.fori_loop(1, 16, scatter, 0)
    image_out(0)
    for c, span, n, ar0, half, ar1, one, ar2 in chains:
        wait_bytes(ar1.at[pl.ds(1, 15)], ar_recv.at[1, c])
        total = half[spot]
        for j in range(1, 16):
            total = total + ar1[j]
        one[...] = total
        ar2[z] = total

        def across(j, _, c=c, one=one, ar2=ar2):
            to = (wide // 8) * 8 + lax.rem(z + j, 8)
            remote(one, ar2.at[z], ar_send.at[2, c], ar_recv.at[2, c], {"wide": to}).start()
            return _

        lax.fori_loop(1, 8, across, 0)
    image_out(1)
    for c, span, n, ar0, half, ar1, one, ar2 in chains:
        wait_bytes(ar2.at[pl.ds(0, 7)], ar_recv.at[2, c])
        total = ar2[0]
        for j in range(1, 8):
            total = total + ar2[j]
        fin[core, spot, span, :] = total

        def spread(j, _, c=c, span=span):
            mine = fin.at[core, spot, span]
            remote(
                mine, mine, ar_send.at[3, c], ar_recv.at[3, c], chip(lax.rem(spot + j, 16))
            ).start()
            return _

        lax.fori_loop(1, 16, spread, 0)
    last = []
    for c, span, n, ar0, half, ar1, one, ar2 in chains:
        wait_bytes(ar1.at[pl.ds(1, 15)], ar_recv.at[3, c])
        done = fin.at[core, :, span]
        last.append(remote(done, done, ar_send.at[4, c], ar_recv.at[4, c], sibling))
        last[-1].start()
    for c in last:
        c.wait_recv()

    wait_bytes(recv.at[pl.ds(0, 63 * 16)], a2a_send.at[0])
    wait_bytes(recv.at[pl.ds(0, 63 * 16)], ret_send.at[0])
    for c in list(ag.values()) + list(rs.values()):
        c.wait_send()
    for c in first + last:
        c.wait_send()
    for c, span, n, ar0, half, ar1, one, ar2 in chains:
        wait_bytes(ar1.at[pl.ds(1, 15)], ar_send.at[1, c])
        wait_bytes(ar2.at[pl.ds(0, 7)], ar_send.at[2, c])
        wait_bytes(ar1.at[pl.ds(1, 15)], ar_send.at[3, c])


def write_out(*refs):
    sem = refs[-1]
    copies = [pltpu.make_async_copy(refs[i], refs[5 + i], sem.at[i]) for i in range(5)]
    for c in copies:
        c.start()
    for c in copies:
        c.wait()


def local(tokens, router, expert_in, expert_out, cotangent):
    images, length, width = tokens.shape
    slots = router.shape[1]
    hidden = expert_in.shape[2]
    rows = images * length
    vm = pltpu.VMEM
    dma = pltpu.SemaphoreType.DMA
    anywhere = pl.BlockSpec(memory_space=pl.ANY)
    outs = (
        jax.ShapeDtypeStruct((rows, width), BF),
        jax.ShapeDtypeStruct((rows, width), BF),
        jax.ShapeDtypeStruct((2, 16, 40, slots), F32),
        jax.ShapeDtypeStruct((width, hidden), BF),
        jax.ShapeDtypeStruct((hidden, width), BF),
    )
    out = pl.pallas_call(
        kernel,
        out_shape=tuple(pltpu.VMEM(o.shape, o.dtype) for o in outs),
        in_specs=[anywhere] * 5,
        out_specs=[pl.BlockSpec(memory_space=pltpu.VMEM)] * 5,
        scratch_shapes=[
            vm((rows, width), BF), vm((width, slots), BF), vm((width, hidden), BF),
            vm((hidden, width), BF), vm((rows, width), BF),
            vm((ROWS, ROWS), BF), vm((ROWS, ROWS), BF),
            vm((rows, slots), F32), vm((rows, slots), F32),
            vm((PH, ROWS, HALF), BF), vm((1024, HALF), BF), vm((1024, HALF), BF),
            vm((PH, 4, 4, EACH, HALF), BF), vm((PH, 4, 4, EACH, HALF), BF),
            vm((PH, 2, 2, EACH, HALF), BF),
            vm((PH, 4, EACH, HALF), BF), vm((PH, 4, EACH, HALF), BF),
            vm((4 * EACH, hidden), F32), vm((4 * EACH, hidden), F32),
            vm((1024, hidden), BF), vm((1024, hidden), BF),
            vm((1024, HALF), BF), vm((1024, HALF), BF),
            vm((8, 128, HALF), BF),
            vm((16, 40, slots), F32), vm((16, 40, slots), F32),
            vm((16, 24, slots), F32), vm((16, 16, slots), F32),
            vm((16, 24, slots), F32), vm((16, 16, slots), F32),
            vm((16, 24, slots), F32), vm((16, 16, slots), F32),
            vm((24, slots), F32), vm((16, slots), F32),
            vm((8, 24, slots), F32), vm((8, 16, slots), F32),
            dma((5,)), dma((2,)), dma((1,)), dma((PH,)),
            dma((PH, 4)), dma((PH, 4)), dma((PH, 6)), dma((PH, 6)),
            dma((1,)), dma((1,)), dma((5, 2)), dma((5, 2)),
        ],
        compiler_params=pltpu.CompilerParams(
            collective_id=0, has_side_effects=True, vmem_limit_bytes=50 * 1024 * 1024
        ),
        cost_estimate=pl.CostEstimate(
            flops=12 * 10**9, bytes_accessed=12 * 10**6, transcendentals=2 * 10**6
        ),
    )(
        tokens.reshape(rows, width), router, expert_in[0], expert_out[0],
        cotangent.reshape(rows, width),
    )
    out = pl.pallas_call(
        write_out,
        out_shape=outs,
        in_specs=[pl.BlockSpec(memory_space=pltpu.VMEM)] * 5,
        out_specs=[anywhere] * 5,
        scratch_shapes=[dma((5,))],
    )(*out)
    mixed, token_grad, router_grad, grad_in, grad_out = out
    return (
        mixed.reshape(images, length, width),
        token_grad.reshape(images, length, width),
        router_grad.reshape(width, slots),
        grad_in[None],
        grad_out[None],
    )


def solution(mesh):
    in_specs = (
        P(("dp", "wide", "narrow"), None, None),
        P(),
        P(("wide", "narrow"), None, "dp"),
        P(("wide", "narrow"), "dp", None),
        P(("dp", "wide", "narrow"), None, None),
    )
    out_specs = (
        P(("dp", "wide", "narrow"), None, None),
        P(("dp", "wide", "narrow"), None, None),
        P(),
        P(("wide", "narrow"), None, "dp"),
        P(("wide", "narrow"), "dp", None),
    )
    return jax.shard_map(local, mesh=mesh, in_specs=in_specs, out_specs=out_specs, check_vma=False)
```

time: 168 us -> 154 us (0.917)
  Pallas kernels: 159 us -> 147 us
  local copies, waits for them, and re-layouts: 8.12 us -> 5.34 us
    pallas_call x1 -> x2, Pallas kernels: 159 us -> 147 us  [the longest x1 142 us: local(): pl.pallas_call(kernel, out_shape=tuple((pltpu.VMEM(o.shape, o.dtype) for...]
    unnamed x13 -> x10, local copies, waits for them, and re-layouts: 8.12 us -> 5.34 us
where the time goes in v3:
time: 154 us
  Pallas kernels  147 us (95%)
  local copies, waits for them, and re-layouts  5.34 us (3%)
    pallas_call x1, Pallas kernels, local(): pl.pallas_call(kernel, out_shape=tuple((pltpu.VMEM(o.shape, o.dtype) for...  142 us
    pallas_call x1, Pallas kernels, local(): pl.pallas_call(write_out, out_shape=outs, in_specs=[pl.BlockSpec(memory_s...  5.74 us
    unnamed x10, local copies, waits for them, and re-layouts  5.34 us

profile of v3, /device:TPU:1, one launch (start us, length us, event | category | flops | bytes accessed | tf_op | source)
XLA Modules:
  0.0 153.6 jit_solution(9249007644206033384)
XLA Ops:
  0.6 141.7 %shard_map.92 = (bf16[512,1280]{1,0:T(8,128)(2,1)S(1)}, bf16[512,1280]{1,0:T(8,128)(2,1)S(1)}, f32[2,16,40,128]{3,2,1,0:T(8,128)S(1)}, bf16[1280,640]{1,0:T(8,128)(2,1)S(1)}, bf16[640,1280]{1,0:T(8,128)(2,1)S(1)}) custom-call(bf16[512,1280]{1,0:T(8,128)(2,1)} %bitcast.13, bf16[1280,128]{1,0:T(8,128)(2,1)} %rout_h.1, bf16[1280,640]{1,0:T(8,128)(2,1)} %bitcast.9, ...), custom_call_target="tpu_custom_call" | custom-call | flops 12000000000 | bytes 12000000 | tf_op jit(solution)/shard_map/pallas_call | solution.py:458
  142.4 0.0 copy-start
  142.4 1.2 copy-done
  143.5 0.0 copy-start.1
  143.5 1.2 copy-done.1
  144.7 0.0 copy-start.2
  144.7 1.1 copy-done.2
  145.8 0.0 copy-start.3
  145.8 1.1 copy-done.3
  146.9 0.0 copy-start.4
  146.9 0.8 copy-done.4
  147.7 5.7 %shard_map.93 = (bf16[512,1280]{1,0:T(8,128)(2,1)}, bf16[512,1280]{1,0:T(8,128)(2,1)}, f32[2,16,40,128]{3,2,1,0:T(8,128)}, bf16[1280,640]{1,0:T(8,128)(2,1)}, bf16[640,1280]{1,0:T(8,128)(2,1)}) custom-call(bf16[512,1280]{1,0:T(8,128)(2,1)} %copy-done.2, bf16[512,1280]{1,0:T(8,128)(2,1)} %copy-done.3, f32[2,16,40,128]{3,2,1,0:T(8,128)} %copy-done.4, ...), custom_call_target="tpu_custom_call" | custom-call | tf_op jit(solution)/shard_map/pallas_call | solution.py:496
Async XLA Ops:
  142.4 1.2 copy-start
  143.5 1.2 copy-start.1
  144.7 1.1 copy-start.2
  145.8 1.1 copy-start.3
  146.9 0.8 copy-start.4

commit v4 on v3

--- a/solution.py
+++ b/solution.py
@@ -14,7 +14,8 @@
 MSG = 64 // PH
 ROWS = 16 * MSG
 EACH = ROWS // 4
-CHAINS = ((0, 24), (24, 16))
+STEPS = ((0, 0), (0, 1), (1, 0), (1, 1), (2, 0), (2, 1), (3, 0), (3, 1))
+OWN = STEPS.index((0, 0)) * MSG
 HALF = 640
 
 
@@ -59,7 +60,7 @@
     tok, rout, win, wout, cot,
     perm, perm_t, disp, comb, stage, send, recv, gath, part, ring_a, ring_b, ring_c,
     pre, back_f, act, hid, ret, back, low,
-    give_v, keep_v, ar0_a, ar0_b, half_a, half_b, ar1_a, ar1_b, one_a, one_b, ar2_a, ar2_b,
+    give_v, keep_v, ar0, half, ar1, one, ar2, whole,
     load_sem, own_sem, a2a_send, a2a_recv, ag_send, ag_recv, rs_send, rs_recv,
     ret_send, ret_recv, ar_send, ar_recv,
 ):
@@ -75,12 +76,13 @@
     def plane(e):
         return {"wide": e // 4, "narrow": lax.rem(e, 4)}
 
-    def place_of(k, sign):
-        j = k % 8
+    def place_of(p, k, sign):
+        dx, dc = STEPS[p]
+        j = lax.rem(k, 8)
         dz = (j % 2) * ((j + 1) // 2) + (1 - j % 2) * (8 - j // 2)
-        px = (x + sign * (k // 16) + 4) % 4
+        px = (x + sign * dx + 4) % 4
         pz = (z + sign * dz + 8) % 8
-        pc = (core + k // 8) % 2
+        pc = (core + dc) % 2
         return (px // 2) * 8 + pz, (px % 2) * 2 + pc
 
     def chip(q):
@@ -115,6 +117,9 @@
         return _
 
     lax.fori_loop(0, 12, greet_far, 0)
+
+    give_v[:, pl.ds(40, 8), :] = jnp.zeros((16, 8, 128), F32)
+    keep_v[:, pl.ds(40, 8), :] = jnp.zeros((16, 8, 128), F32)
 
     def source(r):
         e = r // 16
@@ -155,13 +160,12 @@
     pl.semaphore_wait(barrier, 75)
 
     own = pltpu.make_async_copy(
-        send.at[pl.ds(pl.multiple_of(me * 16, 16), 16)], recv.at[pl.ds(0, 16)], own_sem.at[0]
+        send.at[pl.ds(pl.multiple_of(me * 16, 16), 16)], recv.at[pl.ds(16 * OWN, 16)], own_sem.at[0]
     )
     own.start()
-    for p in range(PH):
-
-        def post(k, _, p=p):
-            w, n = place_of(k, 1)
+    def post_phase(p):
+        def post(k, _):
+            w, n = place_of(p, k, 1)
             pltpu.make_async_remote_copy(
                 src_ref=send.at[pl.ds(pl.multiple_of((w * 4 + n) * 16, 16), 16)],
                 dst_ref=recv.at[pl.ds(pl.multiple_of(k * 16, 16), 16)],
@@ -172,7 +176,10 @@
             ).start()
             return _
 
-        lax.fori_loop(max(MSG * p, 1), MSG * p + MSG, post, 0)
+        lax.fori_loop(MSG * p + (STEPS[p] == (0, 0)), MSG * p + MSG, post, 0)
+
+    for p in range(PH):
+        post_phase(p)
 
     def wait_bytes(ref, sem):
         pltpu.make_async_copy(ref, ref, sem).wait()
@@ -187,9 +194,9 @@
     rs = {}
 
     def stage_a(p):
-        if p == 0:
+        if STEPS[p] == (0, 0):
             own.wait()
-            wait_bytes(recv.at[pl.ds(16, ROWS - 16)], a2a_recv.at[0])
+            wait_bytes(recv.at[pl.ds(0, ROWS - 16)], a2a_recv.at[p])
         else:
             wait_bytes(recv.at[pl.ds(ROWS * p, ROWS)], a2a_recv.at[p])
         rows = dot(perm_t[...], recv[pl.ds(ROWS * p, ROWS), :]).astype(BF)
@@ -261,7 +268,7 @@
         ret[pl.ds(ROWS * p, ROWS), :] = dot(perm[...], total.astype(BF).reshape(ROWS, HALF)).astype(BF)
 
         def post(k, _):
-            w, n = place_of(k, -1)
+            w, n = place_of(p, k, -1)
             pltpu.make_async_remote_copy(
                 src_ref=ret.at[pl.ds(pl.multiple_of(k * 16, 16), 16)],
                 dst_ref=back.at[pl.ds(pl.multiple_of(me * 16, 16), 16)],
@@ -272,10 +279,10 @@
             ).start()
             return _
 
-        lax.fori_loop(max(MSG * p, 1), MSG * p + MSG, post, 0)
-        if p == 0:
+        lax.fori_loop(MSG * p + (STEPS[p] == (0, 0)), MSG * p + MSG, post, 0)
+        if STEPS[p] == (0, 0):
             pltpu.make_async_copy(
-                ret.at[pl.ds(0, 16)], back.at[pl.ds(pl.multiple_of(me * 16, 16), 16)], own_sem.at[1]
+                ret.at[pl.ds(16 * OWN, 16)], back.at[pl.ds(pl.multiple_of(me * 16, 16), 16)], own_sem.at[1]
             ).start()
 
     def grad_first(h):
@@ -305,16 +312,16 @@
             stage_c(t - 2)
         if 0 <= t - 3 < PH:
             stage_d(t - 3)
+        if 0 <= t - 4 < PH:
+            stage_e(t - 4)
         if t == PH + 2:
             grad_first(0)
             grad_first(1)
-        if 0 <= t - 4 < PH:
-            stage_e(t - 4)
     grad_second(0)
     grad_second(1)
 
     pltpu.make_async_copy(
-        ret.at[pl.ds(0, 16)], back.at[pl.ds(pl.multiple_of(me * 16, 16), 16)], own_sem.at[1]
+        ret.at[pl.ds(16 * OWN, 16)], back.at[pl.ds(pl.multiple_of(me * 16, 16), 16)], own_sem.at[1]
     ).wait()
     wait_bytes(back.at[pl.ds(0, 63 * 16)], ret_recv.at[0])
     for g in range(PH):
@@ -340,23 +347,10 @@
         return term.T.reshape(16, 40, 128)
 
     sibling = {"narrow": narrow + 1 - 2 * core}
-    chains = [
-        (c, pl.ds(off, n), n, *refs)
-        for c, ((off, n), refs) in enumerate(
-            zip(
-                CHAINS,
-                ((ar0_a, half_a, ar1_a, one_a, ar2_a), (ar0_b, half_b, ar1_b, one_b, ar2_b)),
-            )
-        )
-    ]
-    give_v[...] = router_half(1 - core)
-    first = []
-    for c, span, n, ar0, half, ar1, one, ar2 in chains:
-        first.append(
-            remote(give_v.at[:, span], ar0, ar_send.at[0, c], ar_recv.at[0, c], sibling)
-        )
-        first[-1].start()
-    keep_v[...] = router_half(core)
+    give_v[:, pl.ds(0, 40), :] = router_half(1 - core)
+    first = remote(give_v, ar0, ar_send.at[0], ar_recv.at[0], sibling)
+    first.start()
+    keep_v[:, pl.ds(0, 40), :] = router_half(core)
 
     def image_out(i):
         rows = pl.ds(i * 256, 256)
@@ -369,66 +363,58 @@
                 dot(dl, low[h * 4 + 2 + i]) + dot_nt(logit[i], rout[cols, :])
             ).astype(BF)
 
-    for c, span, n, ar0, half, ar1, one, ar2 in chains:
-        first[c].wait_recv()
-        half[...] = keep_v[:, span, :] + ar0[...]
-
-        def scatter(j, _, c=c, half=half, ar1=ar1):
-            q = lax.rem(spot + j, 16)
-            remote(half.at[q], ar1.at[j], ar_send.at[1, c], ar_recv.at[1, c], chip(q)).start()
-            return _
-
-        lax.fori_loop(1, 16, scatter, 0)
+    first.wait_recv()
+    half[...] = (keep_v[...] + ar0[...]).astype(BF)
+
+    def scatter(j, _):
+        q = lax.rem(spot + j, 16)
+        remote(half.at[q], ar1.at[j], ar_send.at[1], ar_recv.at[1], chip(q)).start()
+        return _
+
+    lax.fori_loop(1, 16, scatter, 0)
     image_out(0)
-    for c, span, n, ar0, half, ar1, one, ar2 in chains:
-        wait_bytes(ar1.at[pl.ds(1, 15)], ar_recv.at[1, c])
-        total = half[spot]
-        for j in range(1, 16):
-            total = total + ar1[j]
-        one[...] = total
-        ar2[z] = total
-
-        def across(j, _, c=c, one=one, ar2=ar2):
-            to = (wide // 8) * 8 + lax.rem(z + j, 8)
-            remote(one, ar2.at[z], ar_send.at[2, c], ar_recv.at[2, c], {"wide": to}).start()
-            return _
-
-        lax.fori_loop(1, 8, across, 0)
+    wait_bytes(ar1.at[pl.ds(1, 15)], ar_recv.at[1])
+    total = half[spot].astype(F32)
+    for j in range(1, 16):
+        total = total + ar1[j].astype(F32)
+    one[...] = total.astype(BF)
+    ar2[z] = total.astype(BF)
+
+    def across(j, _):
+        to = (wide // 8) * 8 + lax.rem(z + j, 8)
+        remote(one, ar2.at[z], ar_send.at[2], ar_recv.at[2], {"wide": to}).start()
+        return _
+
+    lax.fori_loop(1, 8, across, 0)
     image_out(1)
-    for c, span, n, ar0, half, ar1, one, ar2 in chains:
-        wait_bytes(ar2.at[pl.ds(0, 7)], ar_recv.at[2, c])
-        total = ar2[0]
-        for j in range(1, 8):
-            total = total + ar2[j]
-        fin[core, spot, span, :] = total
-
-        def spread(j, _, c=c, span=span):
-            mine = fin.at[core, spot, span]
-            remote(
-                mine, mine, ar_send.at[3, c], ar_recv.at[3, c], chip(lax.rem(spot + j, 16))
-            ).start()
-            return _
-
-        lax.fori_loop(1, 16, spread, 0)
-    last = []
-    for c, span, n, ar0, half, ar1, one, ar2 in chains:
-        wait_bytes(ar1.at[pl.ds(1, 15)], ar_recv.at[3, c])
-        done = fin.at[core, :, span]
-        last.append(remote(done, done, ar_send.at[4, c], ar_recv.at[4, c], sibling))
-        last[-1].start()
-    for c in last:
-        c.wait_recv()
+    wait_bytes(ar2.at[pl.ds(0, 7)], ar_recv.at[2])
+    total = ar2[0].astype(F32)
+    for j in range(1, 8):
+        total = total + ar2[j].astype(F32)
+    whole[core, spot] = total.astype(BF)
+
+    def spread(j, _):
+        mine = whole.at[core, spot]
+        remote(mine, mine, ar_send.at[3], ar_recv.at[3], chip(lax.rem(spot + j, 16))).start()
+        return _
+
+    lax.fori_loop(1, 16, spread, 0)
+    wait_bytes(ar1.at[pl.ds(1, 15)], ar_recv.at[3])
+    last = remote(whole.at[core], whole.at[core], ar_send.at[4], ar_recv.at[4], sibling)
+    last.start()
+    fin[core] = whole[core].astype(F32)[:, :40, :]
+    last.wait_recv()
+    fin[1 - core] = whole[1 - core].astype(F32)[:, :40, :]
 
     wait_bytes(recv.at[pl.ds(0, 63 * 16)], a2a_send.at[0])
     wait_bytes(recv.at[pl.ds(0, 63 * 16)], ret_send.at[0])
     for c in list(ag.values()) + list(rs.values()):
         c.wait_send()
-    for c in first + last:
-        c.wait_send()
-    for c, span, n, ar0, half, ar1, one, ar2 in chains:
-        wait_bytes(ar1.at[pl.ds(1, 15)], ar_send.at[1, c])
-        wait_bytes(ar2.at[pl.ds(0, 7)], ar_send.at[2, c])
-        wait_bytes(ar1.at[pl.ds(1, 15)], ar_send.at[3, c])
+    first.wait_send()
+    last.wait_send()
+    wait_bytes(ar1.at[pl.ds(1, 15)], ar_send.at[1])
+    wait_bytes(ar2.at[pl.ds(0, 7)], ar_send.at[2])
+    wait_bytes(ar1.at[pl.ds(1, 15)], ar_send.at[3])
 
 
 def write_out(*refs):
@@ -473,15 +459,12 @@
             vm((1024, hidden), BF), vm((1024, hidden), BF),
             vm((1024, HALF), BF), vm((1024, HALF), BF),
             vm((8, 128, HALF), BF),
-            vm((16, 40, slots), F32), vm((16, 40, slots), F32),
-            vm((16, 24, slots), F32), vm((16, 16, slots), F32),
-            vm((16, 24, slots), F32), vm((16, 16, slots), F32),
-            vm((16, 24, slots), F32), vm((16, 16, slots), F32),
-            vm((24, slots), F32), vm((16, slots), F32),
-            vm((8, 24, slots), F32), vm((8, 16, slots), F32),
+            vm((16, 48, slots), F32), vm((16, 48, slots), F32), vm((16, 48, slots), F32),
+            vm((16, 48, slots), BF), vm((16, 48, slots), BF),
+            vm((48, slots), BF), vm((8, 48, slots), BF), vm((2, 16, 48, slots), BF),
             dma((5,)), dma((2,)), dma((1,)), dma((PH,)),
             dma((PH, 4)), dma((PH, 4)), dma((PH, 6)), dma((PH, 6)),
-            dma((1,)), dma((1,)), dma((5, 2)), dma((5, 2)),
+            dma((1,)), dma((1,)), dma((5,)), dma((5,)),
         ],
         compiler_params=pltpu.CompilerParams(
             collective_id=0, has_side_effects=True, vmem_limit_bytes=50 * 1024 * 1024
@@ -499,6 +482,7 @@
         in_specs=[pl.BlockSpec(memory_space=pltpu.VMEM)] * 5,
         out_specs=[anywhere] * 5,
         scratch_shapes=[dma((5,))],
+        compiler_params=pltpu.CompilerParams(vmem_limit_bytes=1024 * 1024),
     )(*out)
     mixed, token_grad, router_grad, grad_in, grad_out = out
     return (

time: 154 us -> 144 us (0.935)
  local copies, waits for them, and re-layouts: 5.34 us -> 0 us
  Pallas kernels: 147 us -> 143 us
    unnamed x10 -> x0, local copies, waits for them, and re-layouts: 5.34 us -> none
    pallas_call x1, Pallas kernels: 5.74 us -> 2.83 us  [local(): pl.pallas_call(write_out, out_shape=outs, in_specs=[pl.BlockSpec(memory_s...]
where the time goes in v4:
time: 144 us
  Pallas kernels  143 us (99%)
    pallas_call x1, Pallas kernels, local(): pl.pallas_call(kernel, out_shape=tuple((pltpu.VMEM(o.shape, o.dtype) for...  141 us

profile of v4, /device:TPU:1, one launch (start us, length us, event | category | flops | bytes accessed | tf_op | source)
XLA Modules:
  0.0 144.3 jit_solution(2795426262761509268)
XLA Ops:
  0.6 140.6 %shard_map.92 = (bf16[512,1280]{1,0:T(8,128)(2,1)S(1)}, bf16[512,1280]{1,0:T(8,128)(2,1)S(1)}, f32[2,16,40,128]{3,2,1,0:T(8,128)S(1)}, bf16[1280,640]{1,0:T(8,128)(2,1)S(1)}, bf16[640,1280]{1,0:T(8,128)(2,1)S(1)}) custom-call(bf16[512,1280]{1,0:T(8,128)(2,1)} %bitcast.13, bf16[1280,128]{1,0:T(8,128)(2,1)} %rout_h.1, bf16[1280,640]{1,0:T(8,128)(2,1)} %bitcast.9, ...), custom_call_target="tpu_custom_call" | custom-call | flops 12000000000 | bytes 12000000 | tf_op jit(solution)/shard_map/pallas_call | solution.py:444
  141.3 2.8 %shard_map.93 = (bf16[512,1280]{1,0:T(8,128)(2,1)}, bf16[512,1280]{1,0:T(8,128)(2,1)}, f32[2,16,40,128]{3,2,1,0:T(8,128)}, bf16[1280,640]{1,0:T(8,128)(2,1)}, bf16[640,1280]{1,0:T(8,128)(2,1)}) custom-call(bf16[512,1280]{1,0:T(8,128)(2,1)S(1)} %get-tuple-element.15.refs_0_, bf16[512,1280]{1,0:T(8,128)(2,1)S(1)} %get-tuple-element.16.refs_1_, ...), custom_call_target="tpu_custom_call" | custom-call | tf_op jit(solution)/shard_map/pallas_call | solution.py:479

commit v5 on v4

--- a/solution.py
+++ b/solution.py
@@ -15,7 +15,6 @@
 ROWS = 16 * MSG
 EACH = ROWS // 4
 STEPS = ((0, 0), (0, 1), (1, 0), (1, 1), (2, 0), (2, 1), (3, 0), (3, 1))
-OWN = STEPS.index((0, 0)) * MSG
 HALF = 640
 
 
@@ -60,9 +59,10 @@
     tok, rout, win, wout, cot,
     perm, perm_t, disp, comb, stage, send, recv, gath, part, ring_a, ring_b, ring_c,
     pre, back_f, act, hid, ret, back, low,
+    early, spare, ret0, home, home_a, home_b, home_c,
     give_v, keep_v, ar0, half, ar1, one, ar2, whole,
     load_sem, own_sem, a2a_send, a2a_recv, ag_send, ag_recv, rs_send, rs_recv,
-    ret_send, ret_recv, ar_send, ar_recv,
+    ret_send, ret_recv, fwd_send, fwd_recv, home_send, home_recv, ar_send, ar_recv,
 ):
     y = lax.axis_index("dp")
     wide = lax.axis_index("wide")
@@ -155,19 +155,37 @@
                         g * EACH // 2 : (g + 1) * EACH // 2, :
                     ]
     for g in range(PH):
-        send[pl.ds(g * ROWS, ROWS), :] = dot(perm[...], stage[g]).astype(BF)
+        send[pl.ds(2 * g, 2)] = dot(perm[...], stage[g]).astype(BF).reshape(2, 4, 16, HALF)
 
     pl.semaphore_wait(barrier, 75)
 
-    own = pltpu.make_async_copy(
-        send.at[pl.ds(pl.multiple_of(me * 16, 16), 16)], recv.at[pl.ds(16 * OWN, 16)], own_sem.at[0]
-    )
+    def wait_bytes(ref, sem):
+        pltpu.make_async_copy(ref, ref, sem).wait()
+
+    def remote(src, dst, s, r, to):
+        return pltpu.make_async_remote_copy(
+            src_ref=src, dst_ref=dst, send_sem=s, recv_sem=r, device_id=to, device_id_type=MESH
+        )
+
+    lo, hi = pl.ds(0, 2), pl.ds(2, 2)
+    ag = {}
+    rs = {}
+
+    line = pl.ds(pl.multiple_of((wide // 8) * 8, 8), 8)
+    front4, rear4 = pl.ds(0, 4), pl.ds(4, 4)
+    ag[0, 0] = remote(send.at[line, narrow], early.at[1], ag_send.at[0, 0], ag_recv.at[0, 0], up)
+    ag[0, 1] = remote(send.at[line, narrow], early.at[3], ag_send.at[0, 1], ag_recv.at[0, 1], down)
+    ag[0, 0].start()
+    ag[0, 1].start()
+
+    own = pltpu.make_async_copy(send.at[wide, narrow], recv.at[pl.ds(0, 16)], own_sem.at[0])
     own.start()
+
     def post_phase(p):
         def post(k, _):
             w, n = place_of(p, k, 1)
             pltpu.make_async_remote_copy(
-                src_ref=send.at[pl.ds(pl.multiple_of((w * 4 + n) * 16, 16), 16)],
+                src_ref=send.at[w, n],
                 dst_ref=recv.at[pl.ds(pl.multiple_of(k * 16, 16), 16)],
                 send_sem=a2a_send.at[0],
                 recv_sem=a2a_recv.at[p],
@@ -176,29 +194,52 @@
             ).start()
             return _
 
-        lax.fori_loop(MSG * p + (STEPS[p] == (0, 0)), MSG * p + MSG, post, 0)
-
-    for p in range(PH):
+        lax.fori_loop(MSG * p + (p == 0), MSG * p + MSG, post, 0)
+
+    for p in (1, 2, 3, 4, 5, 6, 7, 0):
         post_phase(p)
 
-    def wait_bytes(ref, sem):
-        pltpu.make_async_copy(ref, ref, sem).wait()
-
-    def remote(src, dst, s, r, to):
-        return pltpu.make_async_remote_copy(
-            src_ref=src, dst_ref=dst, send_sem=s, recv_sem=r, device_id=to, device_id_type=MESH
-        )
-
-    lo, hi = pl.ds(0, 2), pl.ds(2, 2)
-    ag = {}
-    rs = {}
+    def forward(d):
+        def post(k, _):
+            w, n = place_of(0, k, 1)
+            remote(
+                early.at[d, lax.rem(w, 8)], spare.at[d, k], fwd_send.at[d], fwd_recv.at[d],
+                {"wide": w, "narrow": n},
+            ).start()
+            return _
+
+        lax.fori_loop(1, 8, post, 0)
+
+    def early_relay():
+        ag[0, 0].wait_recv()
+        ag[0, 2] = remote(early.at[1, front4], early.at[2, front4], ag_send.at[0, 2], ag_recv.at[0, 2], up)
+        ag[0, 2].start()
+        ag[0, 1].wait_recv()
+        ag[0, 3] = remote(early.at[3, rear4], early.at[2, rear4], ag_send.at[0, 3], ag_recv.at[0, 3], down)
+        ag[0, 3].start()
+        forward(1)
+        forward(3)
+
+    def early_last():
+        ag[0, 2].wait_recv()
+        ag[0, 3].wait_recv()
+        forward(2)
+        keep = pltpu.make_async_copy(early.at[pl.ds(1, 3), z], spare.at[pl.ds(1, 3), 0], own_sem.at[1])
+        keep.start()
+        keep.wait()
+
+    def early_sort():
+        own.wait()
+        wait_bytes(recv.at[pl.ds(0, ROWS - 16)], a2a_recv.at[0])
+        rows = dot(perm_t[...], recv[pl.ds(0, ROWS), :]).astype(BF)
+        gath[0, :, 0] = rows.reshape(4, EACH, HALF)
+        for d in range(1, 4):
+            wait_bytes(spare.at[d, pl.ds(1, 7)], fwd_recv.at[d])
+            rows = dot(perm_t[...], spare[d].reshape(ROWS, HALF)).astype(BF)
+            gath[0, :, d] = rows.reshape(4, EACH, HALF)
 
     def stage_a(p):
-        if STEPS[p] == (0, 0):
-            own.wait()
-            wait_bytes(recv.at[pl.ds(0, ROWS - 16)], a2a_recv.at[p])
-        else:
-            wait_bytes(recv.at[pl.ds(ROWS * p, ROWS)], a2a_recv.at[p])
+        wait_bytes(recv.at[pl.ds(ROWS * p, ROWS)], a2a_recv.at[p])
         rows = dot(perm_t[...], recv[pl.ds(ROWS * p, ROWS), :]).astype(BF)
         gath[p, :, 0] = rows.reshape(4, EACH, HALF)
         ag[p, 0] = remote(gath.at[p, :, 0], gath.at[p, :, 1], ag_send.at[p, 0], ag_recv.at[p, 0], up)
@@ -214,10 +255,53 @@
         ag[p, 3] = remote(gath.at[p, hi, 3], gath.at[p, hi, 2], ag_send.at[p, 3], ag_recv.at[p, 3], down)
         ag[p, 3].start()
 
+    def early_home():
+        for d in range(4):
+            rows = dot(perm[...], part[0, :, d].reshape(ROWS, HALF)).astype(BF)
+            ret0[d] = rows.reshape(8, 16, HALF)
+
+            def post(k, _, d=d):
+                w, n = place_of(0, k, -1)
+                remote(
+                    ret0.at[d, k], home.at[d, z], home_send.at[0], home_recv.at[0],
+                    {"wide": w, "narrow": n},
+                ).start()
+                return _
+
+            lax.fori_loop(1, 8, post, 0)
+        pltpu.make_async_copy(ret0.at[:, 0], home.at[:, z], own_sem.at[2]).start()
+
+    def late_send():
+        pltpu.make_async_copy(ret0.at[:, 0], home.at[:, z], own_sem.at[2]).wait()
+        wait_bytes(home.at[:, pl.ds(0, 7)], home_recv.at[0])
+        rs[0, 0] = remote(home.at[2, front4], home_a.at[0], rs_send.at[0, 0], rs_recv.at[0, 0], up)
+        rs[0, 1] = remote(home.at[2, rear4], home_a.at[1], rs_send.at[0, 1], rs_recv.at[0, 1], down)
+        rs[0, 2] = remote(home.at[3, rear4], home_b.at[rear4], rs_send.at[0, 2], rs_recv.at[0, 2], up)
+        rs[0, 3] = remote(home.at[1, front4], home_c.at[front4], rs_send.at[0, 3], rs_recv.at[0, 3], down)
+        for j in range(4):
+            rs[0, j].start()
+
+    def late_relay():
+        rs[0, 0].wait_recv()
+        home[3, front4] = (home[3, front4].astype(F32) + home_a[0].astype(F32)).astype(BF)
+        rs[0, 4] = remote(home.at[3, front4], home_b.at[front4], rs_send.at[0, 4], rs_recv.at[0, 4], up)
+        rs[0, 4].start()
+        rs[0, 1].wait_recv()
+        home[1, rear4] = (home[1, rear4].astype(F32) + home_a[1].astype(F32)).astype(BF)
+        rs[0, 5] = remote(home.at[1, rear4], home_c.at[rear4], rs_send.at[0, 5], rs_recv.at[0, 5], down)
+        rs[0, 5].start()
+
+    def late_sum():
+        for j in range(2, 6):
+            rs[0, j].wait_recv()
+        total = home[0].astype(F32) + home_b[...].astype(F32) + home_c[...].astype(F32)
+        back[line, narrow] = total.astype(BF)
+
     def stage_c(p):
-        ag[p, 2].wait_recv()
-        ag[p, 3].wait_recv()
-        if p == 0:
+        if p > 0:
+            ag[p, 2].wait_recv()
+            ag[p, 3].wait_recv()
+        if p == 1:
             loads[3].wait()
             loads[4].wait()
         mine = pl.ds(4 * EACH * p, 4 * EACH)
@@ -244,6 +328,9 @@
             cols = pl.ds(h * HALF, HALF)
             part[p, 2 * h] = dot(act[mine, :], wout[:, cols]).astype(BF).reshape(4, EACH, HALF)
             part[p, 2 * h + 1] = dot_nt(hid[mine, :], win[cols, :]).astype(BF).reshape(4, EACH, HALF)
+        if p == 0:
+            early_home()
+            return
         rs[p, 0] = remote(part.at[p, lo, 2], ring_a.at[p, 0], rs_send.at[p, 0], rs_recv.at[p, 0], up)
         rs[p, 1] = remote(part.at[p, hi, 2], ring_a.at[p, 1], rs_send.at[p, 1], rs_recv.at[p, 1], down)
         rs[p, 2] = remote(part.at[p, hi, 3], ring_b.at[p, hi], rs_send.at[p, 2], rs_recv.at[p, 2], up)
@@ -271,7 +358,7 @@
             w, n = place_of(p, k, -1)
             pltpu.make_async_remote_copy(
                 src_ref=ret.at[pl.ds(pl.multiple_of(k * 16, 16), 16)],
-                dst_ref=back.at[pl.ds(pl.multiple_of(me * 16, 16), 16)],
+                dst_ref=back.at[wide, narrow],
                 send_sem=ret_send.at[0],
                 recv_sem=ret_recv.at[0],
                 device_id={"wide": w, "narrow": n},
@@ -279,11 +366,7 @@
             ).start()
             return _
 
-        lax.fori_loop(MSG * p + (STEPS[p] == (0, 0)), MSG * p + MSG, post, 0)
-        if STEPS[p] == (0, 0):
-            pltpu.make_async_copy(
-                ret.at[pl.ds(16 * OWN, 16)], back.at[pl.ds(pl.multiple_of(me * 16, 16), 16)], own_sem.at[1]
-            ).start()
+        lax.fori_loop(MSG * p, MSG * p + MSG, post, 0)
 
     def grad_first(h):
         total = None
@@ -303,29 +386,37 @@
             total = term if total is None else total + term
         goutv[:, pl.ds(h * HALF, HALF)] = total.astype(BF)
 
-    for t in range(PH + 4):
+    for t in range(1, PH + 4):
         if t < PH:
             stage_a(t)
-        if 0 <= t - 1 < PH:
+        if t == 1:
+            early_relay()
+        if 1 <= t - 1 < PH:
             stage_b(t - 1)
-        if 0 <= t - 2 < PH:
+        if t == 2:
+            early_last()
+        if 1 <= t - 2 < PH:
             stage_c(t - 2)
-        if 0 <= t - 3 < PH:
+        if t == 7:
+            early_sort()
+            stage_c(0)
+        if t == PH + 1:
+            late_send()
+        if 1 <= t - 3 < PH:
             stage_d(t - 3)
-        if 0 <= t - 4 < PH:
+        if 1 <= t - 4 < PH:
             stage_e(t - 4)
         if t == PH + 2:
+            late_relay()
             grad_first(0)
             grad_first(1)
     grad_second(0)
     grad_second(1)
-
-    pltpu.make_async_copy(
-        ret.at[pl.ds(16 * OWN, 16)], back.at[pl.ds(pl.multiple_of(me * 16, 16), 16)], own_sem.at[1]
-    ).wait()
-    wait_bytes(back.at[pl.ds(0, 63 * 16)], ret_recv.at[0])
+    late_sum()
+
+    wait_bytes(back.at[pl.ds(0, 14)], ret_recv.at[0])
     for g in range(PH):
-        rows = dot(perm_t[...], back[pl.ds(g * ROWS, ROWS), :]).astype(BF)
+        rows = dot(perm_t[...], back[pl.ds(2 * g, 2)].reshape(ROWS, HALF)).astype(BF)
         for j in range(8):
             low[j, pl.ds(g * EACH // 2, EACH // 2), :] = rows[j * EACH // 2 : (j + 1) * EACH // 2, :]
     logit = []
@@ -407,7 +498,10 @@
     fin[1 - core] = whole[1 - core].astype(F32)[:, :40, :]
 
     wait_bytes(recv.at[pl.ds(0, 63 * 16)], a2a_send.at[0])
-    wait_bytes(recv.at[pl.ds(0, 63 * 16)], ret_send.at[0])
+    wait_bytes(recv.at[pl.ds(0, 56 * 16)], ret_send.at[0])
+    for d in range(1, 4):
+        wait_bytes(spare.at[d, pl.ds(1, 7)], fwd_send.at[d])
+    wait_bytes(home.at[:, pl.ds(0, 7)], home_send.at[0])
     for c in list(ag.values()) + list(rs.values()):
         c.wait_send()
     first.wait_send()
@@ -451,20 +545,23 @@
             vm((hidden, width), BF), vm((rows, width), BF),
             vm((ROWS, ROWS), BF), vm((ROWS, ROWS), BF),
             vm((rows, slots), F32), vm((rows, slots), F32),
-            vm((PH, ROWS, HALF), BF), vm((1024, HALF), BF), vm((1024, HALF), BF),
+            vm((PH, ROWS, HALF), BF), vm((16, 4, 16, HALF), BF), vm((1024, HALF), BF),
             vm((PH, 4, 4, EACH, HALF), BF), vm((PH, 4, 4, EACH, HALF), BF),
             vm((PH, 2, 2, EACH, HALF), BF),
             vm((PH, 4, EACH, HALF), BF), vm((PH, 4, EACH, HALF), BF),
             vm((4 * EACH, hidden), F32), vm((4 * EACH, hidden), F32),
             vm((1024, hidden), BF), vm((1024, hidden), BF),
-            vm((1024, HALF), BF), vm((1024, HALF), BF),
+            vm((1024, HALF), BF), vm((16, 4, 16, HALF), BF),
             vm((8, 128, HALF), BF),
+            vm((4, 8, 16, HALF), BF), vm((4, 8, 16, HALF), BF),
+            vm((4, 8, 16, HALF), BF), vm((4, 8, 16, HALF), BF),
+            vm((2, 4, 16, HALF), BF), vm((8, 16, HALF), BF), vm((8, 16, HALF), BF),
             vm((16, 48, slots), F32), vm((16, 48, slots), F32), vm((16, 48, slots), F32),
             vm((16, 48, slots), BF), vm((16, 48, slots), BF),
             vm((48, slots), BF), vm((8, 48, slots), BF), vm((2, 16, 48, slots), BF),
-            dma((5,)), dma((2,)), dma((1,)), dma((PH,)),
+            dma((5,)), dma((3,)), dma((1,)), dma((PH,)),
             dma((PH, 4)), dma((PH, 4)), dma((PH, 6)), dma((PH, 6)),
-            dma((1,)), dma((1,)), dma((5,)), dma((5,)),
+            dma((1,)), dma((1,)), dma((4,)), dma((4,)), dma((1,)), dma((1,)), dma((5,)), dma((5,)),
         ],
         compiler_params=pltpu.CompilerParams(
             collective_id=0, has_side_effects=True, vmem_limit_bytes=50 * 1024 * 1024

time: 144 us -> 139 us (0.965)
  Pallas kernels: 143 us -> 138 us
    pallas_call x1, Pallas kernels: 141 us -> 135 us  [local(): pl.pallas_call(kernel, out_shape=tuple((pltpu.VMEM(o.shape, o.dtype) for...]
where the time goes in v5:
time: 139 us
  Pallas kernels  138 us (99%)
    pallas_call x1, Pallas kernels, local(): pl.pallas_call(kernel, out_shape=tuple((pltpu.VMEM(o.shape, o.dtype) for...  135 us
    pallas_call x1, Pallas kernels, local(): pl.pallas_call(write_out, out_shape=outs, in_specs=[pl.BlockSpec(memory_s...  2.83 us

profile of v5, /device:TPU:1, one launch (start us, length us, event | category | flops | bytes accessed | tf_op | source)
XLA Modules:
  0.0 138.8 jit_solution(5807983097456428265)
XLA Ops:
  0.6 135.1 %shard_map.92 = (bf16[512,1280]{1,0:T(8,128)(2,1)S(1)}, bf16[512,1280]{1,0:T(8,128)(2,1)S(1)}, f32[2,16,40,128]{3,2,1,0:T(8,128)S(1)}, bf16[1280,640]{1,0:T(8,128)(2,1)S(1)}, bf16[640,1280]{1,0:T(8,128)(2,1)S(1)}) custom-call(bf16[512,1280]{1,0:T(8,128)(2,1)} %bitcast.13, bf16[1280,128]{1,0:T(8,128)(2,1)} %rout_h.1, bf16[1280,640]{1,0:T(8,128)(2,1)} %bitcast.9, ...), custom_call_target="tpu_custom_call" | custom-call | flops 12000000000 | bytes 12000000 | tf_op jit(solution)/shard_map/pallas_call | solution.py:538
  135.8 2.8 %shard_map.93 = (bf16[512,1280]{1,0:T(8,128)(2,1)}, bf16[512,1280]{1,0:T(8,128)(2,1)}, f32[2,16,40,128]{3,2,1,0:T(8,128)}, bf16[1280,640]{1,0:T(8,128)(2,1)}, bf16[640,1280]{1,0:T(8,128)(2,1)}) custom-call(bf16[512,1280]{1,0:T(8,128)(2,1)S(1)} %get-tuple-element.15.refs_0_, bf16[512,1280]{1,0:T(8,128)(2,1)S(1)} %get-tuple-element.16.refs_1_, ...), custom_call_target="tpu_custom_call" | custom-call | tf_op jit(solution)/shard_map/pallas_call | solution.py:576

commit v6 on v5

--- a/solution.py
+++ b/solution.py
@@ -10,6 +10,8 @@
 MESH = pl.DeviceIdType.MESH
 BF = jnp.bfloat16
 F32 = jnp.float32
+FAR16 = sorted(range(1, 16), key=lambda j: -min(j % 4, 4 - j % 4) - min(j // 4, 4 - j // 4))
+FAR8 = (4, 3, 5, 2, 6, 1, 7)
 PH = 8
 MSG = 64 // PH
 ROWS = 16 * MSG
@@ -400,12 +402,12 @@
         if t == 7:
             early_sort()
             stage_c(0)
-        if t == PH + 1:
-            late_send()
         if 1 <= t - 3 < PH:
             stage_d(t - 3)
         if 1 <= t - 4 < PH:
             stage_e(t - 4)
+        if t == PH + 1:
+            late_send()
         if t == PH + 2:
             late_relay()
             grad_first(0)
@@ -457,12 +459,12 @@
     first.wait_recv()
     half[...] = (keep_v[...] + ar0[...]).astype(BF)
 
-    def scatter(j, _):
-        q = lax.rem(spot + j, 16)
+    def chip_at(j):
+        return lax.rem(y + j // 4, 4) * 4 + lax.rem(x + j % 4, 4)
+
+    for j in FAR16:
+        q = chip_at(j)
         remote(half.at[q], ar1.at[j], ar_send.at[1], ar_recv.at[1], chip(q)).start()
-        return _
-
-    lax.fori_loop(1, 16, scatter, 0)
     image_out(0)
     wait_bytes(ar1.at[pl.ds(1, 15)], ar_recv.at[1])
     total = half[spot].astype(F32)
@@ -471,12 +473,9 @@
     one[...] = total.astype(BF)
     ar2[z] = total.astype(BF)
 
-    def across(j, _):
+    for j in FAR8:
         to = (wide // 8) * 8 + lax.rem(z + j, 8)
         remote(one, ar2.at[z], ar_send.at[2], ar_recv.at[2], {"wide": to}).start()
-        return _
-
-    lax.fori_loop(1, 8, across, 0)
     image_out(1)
     wait_bytes(ar2.at[pl.ds(0, 7)], ar_recv.at[2])
     total = ar2[0].astype(F32)
@@ -484,12 +483,9 @@
         total = total + ar2[j].astype(F32)
     whole[core, spot] = total.astype(BF)
 
-    def spread(j, _):
-        mine = whole.at[core, spot]
-        remote(mine, mine, ar_send.at[3], ar_recv.at[3], chip(lax.rem(spot + j, 16))).start()
-        return _
-
-    lax.fori_loop(1, 16, spread, 0)
+    mine = whole.at[core, spot]
+    for j in FAR16:
+        remote(mine, mine, ar_send.at[3], ar_recv.at[3], chip(chip_at(j))).start()
     wait_bytes(ar1.at[pl.ds(1, 15)], ar_recv.at[3])
     last = remote(whole.at[core], whole.at[core], ar_send.at[4], ar_recv.at[4], sibling)
     last.start()

time: 139 us -> 136 us (0.978)
  Pallas kernels: 138 us -> 135 us
    pallas_call x1, Pallas kernels: 135 us -> 132 us  [local(): pl.pallas_call(kernel, out_shape=tuple((pltpu.VMEM(o.shape, o.dtype) for...]
where the time goes in v6:
time: 136 us
  Pallas kernels  135 us (99%)
    pallas_call x1, Pallas kernels, local(): pl.pallas_call(kernel, out_shape=tuple((pltpu.VMEM(o.shape, o.dtype) for...  132 us
    pallas_call x1, Pallas kernels, local(): pl.pallas_call(write_out, out_shape=outs, in_specs=[pl.BlockSpec(memory_s...  2.83 us

profile of v6, /device:TPU:1, one launch (start us, length us, event | category | flops | bytes accessed | tf_op | source)
XLA Modules:
  0.0 136.0 jit_solution(15392253652247036794)
XLA Ops:
  0.6 132.4 %shard_map.92 = (bf16[512,1280]{1,0:T(8,128)(2,1)S(1)}, bf16[512,1280]{1,0:T(8,128)(2,1)S(1)}, f32[2,16,40,128]{3,2,1,0:T(8,128)S(1)}, bf16[1280,640]{1,0:T(8,128)(2,1)S(1)}, bf16[640,1280]{1,0:T(8,128)(2,1)S(1)}) custom-call(bf16[512,1280]{1,0:T(8,128)(2,1)} %bitcast.13, bf16[1280,128]{1,0:T(8,128)(2,1)} %rout_h.1, bf16[1280,640]{1,0:T(8,128)(2,1)} %bitcast.9, ...), custom_call_target="tpu_custom_call" | custom-call | flops 12000000000 | bytes 12000000 | tf_op jit(solution)/shard_map/pallas_call | solution.py:534
  133.0 2.8 %shard_map.93 = (bf16[512,1280]{1,0:T(8,128)(2,1)}, bf16[512,1280]{1,0:T(8,128)(2,1)}, f32[2,16,40,128]{3,2,1,0:T(8,128)}, bf16[1280,640]{1,0:T(8,128)(2,1)}, bf16[640,1280]{1,0:T(8,128)(2,1)}) custom-call(bf16[512,1280]{1,0:T(8,128)(2,1)S(1)} %get-tuple-element.15.refs_0_, bf16[512,1280]{1,0:T(8,128)(2,1)S(1)} %get-tuple-element.16.refs_1_, ...), custom_call_target="tpu_custom_call" | custom-call | tf_op jit(solution)/shard_map/pallas_call | solution.py:572
